TPU v7x, 768 devices: a whole 4x8x12 slice. The times are simulated.
768 devices in a mesh: dp: 12 (over z), expert: 64 (over x, y, core).
Axes of the slice: x: 4, y: 8, z: 12, core: 2. Of those that a mesh axis runs over, the one named last changes fastest.
Arguments:
- tokens: bfloat16 [1024, 4096], P('expert'), may hold values from -6 to 6
- route: int32 [1024, 8], P('expert'), may hold values from 0 to 63, all different within a row; in each aligned block of 16 rows (0 to 15, 16 to 31, ...) at most 2 rows name the same one
- gate_code: int32 [1024, 8], P('expert'), may hold values from 1 to 999
- cotangent: bfloat16 [1024, 4096], P('expert'), may hold values from -6 to 6
- w_gate: bfloat16 [64, 4096, 1536], P('expert', None, 'dp'), may hold values from -0.09375 to 0.09375
- w_up: bfloat16 [64, 4096, 1536], P('expert', None, 'dp'), may hold values from -0.09375 to 0.09375
- w_down: bfloat16 [64, 1536, 4096], P('expert', 'dp'), may hold values from -0.15625 to 0.15625
Outputs:
- mixed: bfloat16 [1024, 4096], P('expert')
- grad_tokens: bfloat16 [1024, 4096], P('expert')
- grad_gates: float32 [1024, 8], P('expert')
- grad_down: bfloat16 [64, 1536, 4096], P('expert', 'dp')
Inputs may be any that keep to these rules, and one draw needn't show every extreme that they name: `route`: each row names 8 different experts. Within the 16 rows of one device no expert is named more than 2 times, and in some device's rows some expert is named exactly 2 times.
All inputs are finite; a program needn't handle non-finite values.
Results may differ from a plain program's by a relative error of at most 0.023.
Values may be sent and summed in bfloat16 or wider, within the bound.
A program may use at most 64 MiB of HBM per device.

v0:
```python
import jax
import jax.numpy as jnp
from jax import lax
from jax.sharding import PartitionSpec as P


def local(tokens, route, gate_code, cotangent, w_gate, w_up, w_down):
    n_expert = lax.axis_size("expert")
    tok_rows, width = tokens.shape
    top_k = route.shape[1]
    capacity = min(tok_rows, max(2, 4 * tok_rows * top_k // (3 * n_expert)))
    slot_count = n_expert * capacity
    codes = gate_code.astype(jnp.float32)
    gates = codes / jnp.sum(codes, axis=1, keepdims=True)
    flat_route = route.reshape(-1)
    onehot = (flat_route[:, None] == jnp.arange(n_expert, dtype=jnp.int32)[None, :]).astype(
        jnp.int32
    )
    before = jnp.cumsum(onehot, axis=0) - onehot
    slot_rank = jnp.sum(before * onehot, axis=1)
    slot_index = flat_route * capacity + slot_rank
    placing = (slot_index[None, :] == jnp.arange(slot_count, dtype=jnp.int32)[:, None]).astype(
        jnp.bfloat16
    )
    token_pick = jnp.sum(placing.reshape(slot_count, tok_rows, top_k), axis=2)
    send_rows = jnp.dot(token_pick, tokens, preferred_element_type=jnp.float32).astype(jnp.bfloat16)
    pair_grad = (
        gates.reshape(-1)[:, None] * jnp.repeat(cotangent, top_k, axis=0).astype(jnp.float32)
    ).astype(jnp.bfloat16)
    send_grad = jnp.dot(placing, pair_grad, preferred_element_type=jnp.float32).astype(jnp.bfloat16)
    shape3 = (n_expert, capacity, width)
    recv_rows, recv_grad = (
        lax.all_to_all(
            send_rows.reshape(shape3), "expert", split_axis=0, concat_axis=0, tiled=True
        ),
        lax.all_to_all(
            send_grad.reshape(shape3), "expert", split_axis=0, concat_axis=0, tiled=True
        ),
    )
    recv_rows = recv_rows.reshape(slot_count, width)
    recv_grad = recv_grad.reshape(slot_count, width)
    weight_gate = w_gate[0]
    weight_up = w_up[0]
    weight_down = w_down[0]
    gate_pre = jnp.dot(recv_rows, weight_gate, preferred_element_type=jnp.float32)
    up_pre = jnp.dot(recv_rows, weight_up, preferred_element_type=jnp.float32)
    sigma = jax.nn.sigmoid(gate_pre)
    silu_gate = gate_pre * sigma
    hidden = (silu_gate * up_pre).astype(jnp.bfloat16)
    expert_out = jnp.dot(hidden, weight_down, preferred_element_type=jnp.float32).astype(
        jnp.bfloat16
    )
    grad_hidden = lax.dot_general(
        recv_grad, weight_down, (((1,), (1,)), ((), ())), preferred_element_type=jnp.float32
    )
    grad_gate_pre = (grad_hidden * up_pre * sigma * (1.0 + gate_pre * (1.0 - sigma))).astype(
        jnp.bfloat16
    )
    grad_up_pre = (grad_hidden * silu_gate).astype(jnp.bfloat16)
    input_part = (
        lax.dot_general(
            grad_gate_pre, weight_gate, (((1,), (1,)), ((), ())), preferred_element_type=jnp.float32
        )
        + lax.dot_general(
            grad_up_pre, weight_up, (((1,), (1,)), ((), ())), preferred_element_type=jnp.float32
        )
    ).astype(jnp.bfloat16)
    grad_weight = lax.dot_general(
        hidden, recv_grad, (((0,), (0,)), ((), ())), preferred_element_type=jnp.float32
    ).astype(jnp.bfloat16)
    cot_float = cotangent.astype(jnp.float32)
    back_out, back_input = (
        lax.all_to_all(
            expert_out.reshape(shape3), "expert", split_axis=0, concat_axis=0, tiled=True
        ),
        lax.all_to_all(
            input_part.reshape(shape3), "expert", split_axis=0, concat_axis=0, tiled=True
        ),
    )
    pair_out = lax.dot_general(
        placing,
        back_out.reshape(slot_count, width),
        (((0,), (0,)), ((), ())),
        preferred_element_type=jnp.float32,
    )
    pair_input = lax.dot_general(
        placing,
        back_input.reshape(slot_count, width),
        (((0,), (0,)), ((), ())),
        preferred_element_type=jnp.float32,
    )
    total_out, total_input = (
        lax.psum(pair_out.astype(jnp.bfloat16), "dp").astype(jnp.float32),
        lax.psum(pair_input.astype(jnp.bfloat16), "dp").astype(jnp.float32),
    )
    out3 = total_out.reshape(tok_rows, top_k, width)
    mixed = jnp.sum(gates[:, :, None] * out3, axis=1)
    grad_gates = jnp.sum(cot_float[:, None, :] * out3, axis=2)
    grad_tokens = jnp.sum(total_input.reshape(tok_rows, top_k, width), axis=1)
    return (
        mixed.astype(jnp.bfloat16),
        grad_tokens.astype(jnp.bfloat16),
        grad_gates,
        grad_weight[None],
    )


def solution(mesh):
    return jax.shard_map(
        local,
        mesh=mesh,
        in_specs=(
            P("expert", None),
            P("expert", None),
            P("expert", None),
            P("expert", None),
            P("expert", None, "dp"),
            P("expert", None, "dp"),
            P("expert", "dp", None),
        ),
        out_specs=(
            P("expert", None),
            P("expert", None),
            P("expert", None),
            P("expert", "dp", None),
        ),
        check_vma=False,
    )
```

profile of v0, /device:TPU:6, one launch (start us, length us, event | category | flops | bytes accessed | tf_op | source)
XLA Modules:
  0.0 304.3 jit_solution(6019113514174507478)
XLA Ops:
  10.2 1.5 reshape.72
  11.7 13.9 %all-to-all-start = ((bf16[64,2,4096]{2,1,0:T(2,128)(2,1)}), bf16[64,2,4096]{2,1,0:T(2,128)(2,1)S(1)}, u32[]{:S(2)}, u32[]{:S(2)}) async-start(bf16[64,2,4096]{2,1,0:T(2,128)(2,1)} %reshape.72), calls=%async_computation | async-start | bytes 2097152 | tf_op jit(solution)/shard_map/all_to_all | solution.py:33
  26.3 1.5 reshape.77
  27.8 24.4 %all-to-all-done = bf16[64,2,4096]{2,1,0:T(2,128)(2,1)S(1)} async-done(((bf16[64,2,4096]{2,1,0:T(2,128)(2,1)}), bf16[64,2,4096]{2,1,0:T(2,128)(2,1)S(1)}, u32[]{:S(2)}, u32[]{:S(2)}) %all-to-all-start) | async-done | bytes 1048608 | tf_op jit(solution)/shard_map/all_to_all | solution.py:33
  53.2 8.3 %all-to-all-start.2 = ((bf16[64,2,4096]{2,1,0:T(2,128)(2,1)}), bf16[64,2,4096]{2,1,0:T(2,128)(2,1)}, u32[]{:S(2)}, u32[]{:S(2)}) async-start(bf16[64,2,4096]{2,1,0:T(2,128)(2,1)} %reshape.77), calls=%async_computation.2 | async-start | bytes 2097152 | tf_op jit(solution)/shard_map/all_to_all | solution.py:36
  61.5 1.5 reshape.73
  64.5 23.6 %all-to-all-done.2 = bf16[64,2,4096]{2,1,0:T(2,128)(2,1)} async-done(((bf16[64,2,4096]{2,1,0:T(2,128)(2,1)}), bf16[64,2,4096]{2,1,0:T(2,128)(2,1)}, u32[]{:S(2)}, u32[]{:S(2)}) %all-to-all-start.2) | async-done | bytes 1048608 | tf_op jit(solution)/shard_map/all_to_all | solution.py:36
  88.1 1.5 reshape.78
  89.5 1.7 fusion.8
  91.7 1.4 fusion
  93.1 2.6 reshape.79
  95.7 8.3 %all-to-all-start.3 = ((bf16[64,2,4096]{2,1,0:T(2,128)(2,1)}), bf16[64,2,4096]{2,1,0:T(2,128)(2,1)}, u32[]{:S(2)}, u32[]{:S(2)}) async-start(bf16[64,2,4096]{2,1,0:T(2,128)(2,1)} %reshape.79), calls=%async_computation.3 | async-start | bytes 2097152 | tf_op jit(solution)/shard_map/all_to_all | solution.py:76
  105.4 2.5 reshape.74
  108.0 22.6 %all-to-all-done.3 = bf16[64,2,4096]{2,1,0:T(2,128)(2,1)} async-done(((bf16[64,2,4096]{2,1,0:T(2,128)(2,1)}), bf16[64,2,4096]{2,1,0:T(2,128)(2,1)}, u32[]{:S(2)}, u32[]{:S(2)}) %all-to-all-start.3) | async-done | bytes 1048608 | tf_op jit(solution)/shard_map/all_to_all | solution.py:76
  130.6 8.3 %all-to-all-start.1 = ((bf16[64,2,4096]{2,1,0:T(2,128)(2,1)}), bf16[64,2,4096]{2,1,0:T(2,128)(2,1)}, u32[]{:S(2)}, u32[]{:S(2)}) async-start(bf16[64,2,4096]{2,1,0:T(2,128)(2,1)} %reshape.74), calls=%async_computation.1 | async-start | bytes 2097152 | tf_op jit(solution)/shard_map/all_to_all | solution.py:73
  139.1 1.5 reshape.80
  140.6 1.5 fusion.1
  142.1 23.4 %all-to-all-done.1 = bf16[64,2,4096]{2,1,0:T(2,128)(2,1)} async-done(((bf16[64,2,4096]{2,1,0:T(2,128)(2,1)}), bf16[64,2,4096]{2,1,0:T(2,128)(2,1)}, u32[]{:S(2)}, u32[]{:S(2)}) %all-to-all-start.1) | async-done | bytes 1048608 | tf_op jit(solution)/shard_map/all_to_all | solution.py:73
  165.5 1.5 reshape.75
  166.9 1.5 convolution_convert_fusion.3
  168.4 1.4 fusion.2
  169.8 121.3 %all-reduce.3.cloned.1.call-done = (bf16[128,4096]{1,0:T(8,128)(2,1)}, bf16[16,8,4096]{2,1,0:T(8,128)(2,1)}) async-done(((bf16[128,4096]{1,0:T(8,128)(2,1)}, bf16[16,8,4096]{2,1,0:T(8,128)(2,1)}), (bf16[128,4096]{1,0:T(8,128)(2,1)}, bf16[16,8,4096]{2,1,0:T(8,128)(2,1)})) %all-reduce.3.cloned.1.call-update) | async-done | bytes 2097168 | tf_op jit(solution)/shard_map/psum | solution.py:93
  291.1 1.6 fusion.6
  292.7 2.7 fusion.4
  (41 shorter events, 10.3 us)
Async XLA Ops:
  7.2 56.2 %copy-start = (bf16[1,4096,128]{2,1,0:T(8,128)(2,1)S(1)}, bf16[1,4096,128]{2,1,0:T(8,128)(2,1)}, u32[]{:S(2)}) copy-start(bf16[1,4096,128]{2,1,0:T(8,128)(2,1)} %param.12) | copy-start | bytes 3145732
  10.1 15.4 %copy-start.6 = (bf16[16,4096]{1,0:T(8,128)(2,1)S(1)}, bf16[16,4096]{1,0:T(8,128)(2,1)}, u32[]{:S(2)}) copy-start(bf16[16,4096]{1,0:T(8,128)(2,1)} %param.10) | copy-start | bytes 393220
  10.1 15.5 %copy-start.7 = (s32[16,8]{0,1:T(8,128)S(1)}, s32[16,8]{0,1:T(8,128)}, u32[]{:S(2)}) copy-start(s32[16,8]{0,1:T(8,128)} %param.9) | copy-start | bytes 1540
  11.7 40.6 %all-to-all-start = ((bf16[64,2,4096]{2,1,0:T(2,128)(2,1)}), bf16[64,2,4096]{2,1,0:T(2,128)(2,1)S(1)}, u32[]{:S(2)}, u32[]{:S(2)}) async-start(bf16[64,2,4096]{2,1,0:T(2,128)(2,1)} %reshape.72), calls=%async_computation | async-start | bytes 2097152 | tf_op jit(solution)/shard_map/all_to_all | solution.py:33
  27.8 35.1 %copy-start.1 = (bf16[1,4096,128]{2,1,0:T(8,128)(2,1)S(1)}, bf16[1,4096,128]{2,1,0:T(8,128)(2,1)}, u32[]{:S(2)}) copy-start(bf16[1,4096,128]{2,1,0:T(8,128)(2,1)} %param.11) | copy-start | bytes 3145732
  52.2 1.0 copy-start.3
  53.2 34.9 %all-to-all-start.2 = ((bf16[64,2,4096]{2,1,0:T(2,128)(2,1)}), bf16[64,2,4096]{2,1,0:T(2,128)(2,1)}, u32[]{:S(2)}, u32[]{:S(2)}) async-start(bf16[64,2,4096]{2,1,0:T(2,128)(2,1)} %reshape.77), calls=%async_computation.2 | async-start | bytes 2097152 | tf_op jit(solution)/shard_map/all_to_all | solution.py:36
  89.5 1.7 copy-start.5
  93.1 10.9 %copy-start.2 = (bf16[1,128,4096]{2,1,0:T(8,128)(2,1)S(1)}, bf16[1,128,4096]{2,1,0:T(8,128)(2,1)}, u32[]{:S(2)}) copy-start(bf16[1,128,4096]{2,1,0:T(8,128)(2,1)} %param.13) | copy-start | bytes 3145732
  95.7 34.9 %all-to-all-start.3 = ((bf16[64,2,4096]{2,1,0:T(2,128)(2,1)}), bf16[64,2,4096]{2,1,0:T(2,128)(2,1)}, u32[]{:S(2)}, u32[]{:S(2)}) async-start(bf16[64,2,4096]{2,1,0:T(2,128)(2,1)} %reshape.79), calls=%async_computation.3 | async-start | bytes 2097152 | tf_op jit(solution)/shard_map/all_to_all | solution.py:76
  130.6 34.9 %all-to-all-start.1 = ((bf16[64,2,4096]{2,1,0:T(2,128)(2,1)}), bf16[64,2,4096]{2,1,0:T(2,128)(2,1)}, u32[]{:S(2)}, u32[]{:S(2)}) async-start(bf16[64,2,4096]{2,1,0:T(2,128)(2,1)} %reshape.74), calls=%async_computation.1 | async-start | bytes 2097152 | tf_op jit(solution)/shard_map/all_to_all | solution.py:73
  138.9 152.2 %all-reduce.3.cloned.1.call-start = ((), (), s32[]{:S(2)}) async-start(), calls=%async_computation.4 | async-start | bytes 4194304 | tf_op jit(solution)/shard_map/psum | solution.py:93
  291.1 5.0 %copy-start.4 = (bf16[16,8,4096]{2,1,0:T(8,128)(2,1)S(1)}, bf16[16,8,4096]{2,1,0:T(8,128)(2,1)}, u32[]{:S(2)}) copy-start(bf16[16,8,4096]{2,1,0:T(8,128)(2,1)} %get-tuple-element.17) | copy-start | bytes 3145732
Sparse Core Ops, SparseCore 0:
  168.5 122.5 all-reduce.2
where the time goes:
time: 305 us; the launch traced here: 304 us
  waiting for transfers between devices  215 us (70%)
  starting transfers between devices  39 us (13%)
  local copies, waits for them, and re-layouts  17 us (6%)
  between operations  14.3 us (5%)
  matrix products  12.6 us (4%)
  other arithmetic  6.25 us (2%)
    psum x1, waiting for transfers between devices, local(): lax.psum(pair_out.astype(jnp.bfloat16), 'dp').astype(jnp.float32)  121 us
    all_to_all x1, waiting for transfers between devices, local(): lax.all_to_all(send_rows.reshape(shape3), 'expert', split_axis=0, concat_...  24.4 us
    all_to_all x1, waiting for transfers between devices, local(): lax.all_to_all(send_grad.reshape(shape3), 'expert', split_axis=0, concat_...  23.6 us
    all_to_all x1, waiting for transfers between devices, local(): lax.all_to_all(expert_out.reshape(shape3), 'expert', split_axis=0, concat...  23.4 us
    all_to_all x1, waiting for transfers between devices, local(): lax.all_to_all(input_part.reshape(shape3), 'expert', split_axis=0, concat...  22.6 us
    all_to_all x1, starting transfers between devices, local(): lax.all_to_all(send_rows.reshape(shape3), 'expert', split_axis=0, concat_...  13.9 us
    all_to_all x1, starting transfers between devices, local(): lax.all_to_all(send_grad.reshape(shape3), 'expert', split_axis=0, concat_...  8.29 us
    all_to_all x1, starting transfers between devices, local(): lax.all_to_all(expert_out.reshape(shape3), 'expert', split_axis=0, concat...  8.29 us
  transfers between devices with their start and end apart: 5, of which 5 were waited for; matrix products, arithmetic and copies ran while one was open for 4% of the time, Pallas kernels for 0%

commit v1 on v0

--- a/solution.py
+++ b/solution.py
@@ -89,20 +89,16 @@
         (((0,), (0,)), ((), ())),
         preferred_element_type=jnp.float32,
     )
-    total_out, total_input = (
-        lax.psum(pair_out.astype(jnp.bfloat16), "dp").astype(jnp.float32),
-        lax.psum(pair_input.astype(jnp.bfloat16), "dp").astype(jnp.float32),
+    out3 = pair_out.reshape(tok_rows, top_k, width)
+    mixed_part = jnp.sum(gates[:, :, None] * out3, axis=1).astype(jnp.bfloat16)
+    gates_part = jnp.sum(cot_float[:, None, :] * out3, axis=2)
+    tokens_part = jnp.sum(pair_input.reshape(tok_rows, top_k, width), axis=1).astype(jnp.bfloat16)
+    mixed, grad_tokens, grad_gates = (
+        lax.psum(mixed_part, "dp"),
+        lax.psum(tokens_part, "dp"),
+        lax.psum(gates_part, "dp"),
     )
-    out3 = total_out.reshape(tok_rows, top_k, width)
-    mixed = jnp.sum(gates[:, :, None] * out3, axis=1)
-    grad_gates = jnp.sum(cot_float[:, None, :] * out3, axis=2)
-    grad_tokens = jnp.sum(total_input.reshape(tok_rows, top_k, width), axis=1)
-    return (
-        mixed.astype(jnp.bfloat16),
-        grad_tokens.astype(jnp.bfloat16),
-        grad_gates,
-        grad_weight[None],
-    )
+    return mixed, grad_tokens, grad_gates, grad_weight[None]
 
 
 def solution(mesh):

time: 305 us -> 286 us (0.938)
  waiting for transfers between devices: 215 us -> 169 us
  blocking collectives: 0 us -> 30.6 us
  other arithmetic: 6.25 us -> 0.61 us
    psum x1, waiting for transfers between devices: 121 us -> 80.8 us  [local(): lax.psum(mixed_part, 'dp')]
    psum x0 -> x1, blocking collectives: none -> 30.6 us  [local(): lax.psum(gates_part, 'dp')]
    reduce_sum x3 -> x0, other arithmetic: 5.64 us -> none  [the longest x1 2.69 us: local(): mixed = jnp.sum(gates[:, :, None] * out3, axis=1)]
    unnamed x18, local copies, waits for them, and re-layouts: 2.53 us -> 5.65 us
  transfers between devices with their start and end apart: 5 -> 5, of which waited for: 5 -> 5; matrix products, arithmetic and copies ran while one was open for 4% -> 7% of each run, Pallas kernels for 0% -> 0%
where the time goes in v1:
time: 286 us; the launch traced here: 285 us
  waiting for transfers between devices  169 us (59%)
  starting transfers between devices  38.6 us (13%)
  blocking collectives  30.6 us (11%)
  local copies, waits for them, and re-layouts  18.4 us (6%)
  between operations  14.3 us (5%)
  matrix products  13.4 us (5%)
    psum x1, waiting for transfers between devices, local(): lax.psum(mixed_part, 'dp')  80.8 us
    psum x1, blocking collectives, local(): lax.psum(gates_part, 'dp')  30.6 us
    all_to_all x1, waiting for transfers between devices, local(): lax.all_to_all(send_rows.reshape(shape3), 'expert', split_axis=0, concat_...  24.4 us
    all_to_all x1, waiting for transfers between devices, local(): lax.all_to_all(send_grad.reshape(shape3), 'expert', split_axis=0, concat_...  21.6 us
    all_to_all x1, waiting for transfers between devices, local(): lax.all_to_all(input_part.reshape(shape3), 'expert', split_axis=0, concat...  21.4 us
    all_to_all x1, waiting for transfers between devices, local(): lax.all_to_all(expert_out.reshape(shape3), 'expert', split_axis=0, concat...  21 us
    all_to_all x1, starting transfers between devices, local(): lax.all_to_all(send_rows.reshape(shape3), 'expert', split_axis=0, concat_...  13.9 us
    all_to_all x1, starting transfers between devices, local(): lax.all_to_all(expert_out.reshape(shape3), 'expert', split_axis=0, concat...  8.29 us
  transfers between devices with their start and end apart: 5, of which 5 were waited for; matrix products, arithmetic and copies ran while one was open for 7% of the time, Pallas kernels for 0%

profile of v1, /device:TPU:6, one launch (start us, length us, event | category | flops | bytes accessed | tf_op | source)
XLA Modules:
  0.0 285.0 jit_solution(1879699951546637319)
XLA Ops:
  8.8 1.4 convolution_convert_fusion.3
  10.2 1.5 reshape.86
  11.7 13.9 %all-to-all-start = ((bf16[64,2,4096]{2,1,0:T(2,128)(2,1)}), bf16[64,2,4096]{2,1,0:T(2,128)(2,1)S(1)}, u32[]{:S(2)}, u32[]{:S(2)}) async-start(bf16[64,2,4096]{2,1,0:T(2,128)(2,1)} %reshape.86), calls=%async_computation | async-start | bytes 2097152 | tf_op jit(solution)/shard_map/all_to_all | solution.py:33
  26.3 1.5 reshape.90
  27.8 24.4 %all-to-all-done = bf16[64,2,4096]{2,1,0:T(2,128)(2,1)S(1)} async-done(((bf16[64,2,4096]{2,1,0:T(2,128)(2,1)}), bf16[64,2,4096]{2,1,0:T(2,128)(2,1)S(1)}, u32[]{:S(2)}, u32[]{:S(2)}) %all-to-all-start) | async-done | bytes 1048608 | tf_op jit(solution)/shard_map/all_to_all | solution.py:33
  53.2 8.3 %all-to-all-start.2 = ((bf16[64,2,4096]{2,1,0:T(2,128)(2,1)}), bf16[64,2,4096]{2,1,0:T(2,128)(2,1)}, u32[]{:S(2)}, u32[]{:S(2)}) async-start(bf16[64,2,4096]{2,1,0:T(2,128)(2,1)} %reshape.90), calls=%async_computation.2 | async-start | bytes 2097152 | tf_op jit(solution)/shard_map/all_to_all | solution.py:36
  61.5 1.5 reshape.87
  64.9 1.5 reshape.88
  66.4 21.6 %all-to-all-done.2 = bf16[64,2,4096]{2,1,0:T(2,128)(2,1)} async-done(((bf16[64,2,4096]{2,1,0:T(2,128)(2,1)}), bf16[64,2,4096]{2,1,0:T(2,128)(2,1)}, u32[]{:S(2)}, u32[]{:S(2)}) %all-to-all-start.2) | async-done | bytes 1048608 | tf_op jit(solution)/shard_map/all_to_all | solution.py:36
  88.0 8.3 %all-to-all-start.1 = ((bf16[64,2,4096]{2,1,0:T(2,128)(2,1)}), bf16[64,2,4096]{2,1,0:T(2,128)(2,1)}, u32[]{:S(2)}, u32[]{:S(2)}) async-start(bf16[64,2,4096]{2,1,0:T(2,128)(2,1)} %reshape.88), calls=%async_computation.1 | async-start | bytes 2097152 | tf_op jit(solution)/shard_map/all_to_all | solution.py:73
  96.3 1.5 reshape.91
  97.8 1.7 fusion.4
  100.4 1.5 reshape.92
  101.9 21.0 %all-to-all-done.1 = bf16[64,2,4096]{2,1,0:T(2,128)(2,1)} async-done(((bf16[64,2,4096]{2,1,0:T(2,128)(2,1)}), bf16[64,2,4096]{2,1,0:T(2,128)(2,1)}, u32[]{:S(2)}, u32[]{:S(2)}) %all-to-all-start.1) | async-done | bytes 1048608 | tf_op jit(solution)/shard_map/all_to_all | solution.py:73
  122.9 8.1 %all-to-all-start.3 = ((bf16[64,2,4096]{2,1,0:T(2,128)(2,1)}), bf16[64,2,4096]{2,1,0:T(2,128)(2,1)S(1)}, u32[]{:S(2)}, u32[]{:S(2)}) async-start(bf16[64,2,4096]{2,1,0:T(2,128)(2,1)} %reshape.92), calls=%async_computation.3 | async-start | bytes 2097152 | tf_op jit(solution)/shard_map/all_to_all | solution.py:76
  131.1 2.2 reshape.94
  133.3 2.9 %multiply_reduce_fusion = (f32[16,8]{1,0:T(8,128)S(1)}, bf16[16,4096]{1,0:T(8,128)(2,1)}) fusion(f32[16,4096]{1,0:T(8,128)S(1)} %convert_element_type.60, f32[16,8]{1,0:T(8,128)S(1)} %copy.24, bf16[128,4096,1]{1,0,2:T(8,128)(2,1)} %reshape.94, s32[16,8]{1,0:T(8,128)S(1)} %multiply_add_fusion), kind=kOutput, calls=%fused_computation.9 | convolution fusion | flops 136265600 | bytes 1443328 | tf_op jit(solution)/shard_map/dot_general | solution.py:80
  136.3 21.4 %all-to-all-done.3 = bf16[64,2,4096]{2,1,0:T(2,128)(2,1)S(1)} async-done(((bf16[64,2,4096]{2,1,0:T(2,128)(2,1)}), bf16[64,2,4096]{2,1,0:T(2,128)(2,1)S(1)}, u32[]{:S(2)}, u32[]{:S(2)}) %all-to-all-start.3) | async-done | bytes 1048608 | tf_op jit(solution)/shard_map/all_to_all | solution.py:76
  158.9 2.7 convolution_reduce_fusion
  161.6 1.4 fusion.1
  163.0 30.6 %psum.23 = f32[16,8]{1,0:T(8,128)S(1)} all-reduce(f32[16,8]{1,0:T(8,128)S(1)} %get-tuple-element.12), channel_id=1, replica_groups=mesh['dp'=12,'expert'=64] {'dp'}, use_global_device_ids=true, to_apply=%region_9.10 | all-reduce | flops 128 | bytes 1024 | tf_op jit(solution)/shard_map/psum | solution.py:99
  194.2 80.8 %all-reduce.3.cloned.1.call-done = (bf16[16,4096]{1,0:T(8,128)(2,1)}, bf16[16,4096]{1,0:T(8,128)(2,1)}) async-done(((bf16[16,4096]{1,0:T(8,128)(2,1)}, bf16[16,4096]{1,0:T(8,128)(2,1)}), (bf16[16,4096]{1,0:T(8,128)(2,1)}, bf16[16,4096]{1,0:T(8,128)(2,1)})) %all-reduce.3.cloned.1.call-update) | async-done | bytes 262160 | tf_op jit(solution)/shard_map/psum | solution.py:97
  275.0 1.6 copy.31
  276.6 1.6 copy.32
  (38 shorter events, 8.0 us)
Async XLA Ops:
  7.2 56.2 %copy-start = (bf16[1,4096,128]{2,1,0:T(8,128)(2,1)S(1)}, bf16[1,4096,128]{2,1,0:T(8,128)(2,1)}, u32[]{:S(2)}) copy-start(bf16[1,4096,128]{2,1,0:T(8,128)(2,1)} %param.12) | copy-start | bytes 3145732
  10.1 15.4 %copy-start.6 = (s32[16,8]{0,1:T(8,128)S(1)}, s32[16,8]{0,1:T(8,128)}, u32[]{:S(2)}) copy-start(s32[16,8]{0,1:T(8,128)} %param.9) | copy-start | bytes 1540
  10.1 15.6 %copy-start.5 = (bf16[16,4096]{1,0:T(8,128)(2,1)S(1)}, bf16[16,4096]{1,0:T(8,128)(2,1)}, u32[]{:S(2)}) copy-start(bf16[16,4096]{1,0:T(8,128)(2,1)} %param.10) | copy-start | bytes 393220
  11.7 40.6 %all-to-all-start = ((bf16[64,2,4096]{2,1,0:T(2,128)(2,1)}), bf16[64,2,4096]{2,1,0:T(2,128)(2,1)S(1)}, u32[]{:S(2)}, u32[]{:S(2)}) async-start(bf16[64,2,4096]{2,1,0:T(2,128)(2,1)} %reshape.86), calls=%async_computation | async-start | bytes 2097152 | tf_op jit(solution)/shard_map/all_to_all | solution.py:33
  27.8 35.1 %copy-start.1 = (bf16[1,4096,128]{2,1,0:T(8,128)(2,1)S(1)}, bf16[1,4096,128]{2,1,0:T(8,128)(2,1)}, u32[]{:S(2)}) copy-start(bf16[1,4096,128]{2,1,0:T(8,128)(2,1)} %param.11) | copy-start | bytes 3145732
  52.2 1.0 copy-start.3
  53.2 34.9 %all-to-all-start.2 = ((bf16[64,2,4096]{2,1,0:T(2,128)(2,1)}), bf16[64,2,4096]{2,1,0:T(2,128)(2,1)}, u32[]{:S(2)}, u32[]{:S(2)}) async-start(bf16[64,2,4096]{2,1,0:T(2,128)(2,1)} %reshape.90), calls=%async_computation.2 | async-start | bytes 2097152 | tf_op jit(solution)/shard_map/all_to_all | solution.py:36
  63.0 1.5 copy-start.2
  88.0 34.9 %all-to-all-start.1 = ((bf16[64,2,4096]{2,1,0:T(2,128)(2,1)}), bf16[64,2,4096]{2,1,0:T(2,128)(2,1)}, u32[]{:S(2)}, u32[]{:S(2)}) async-start(bf16[64,2,4096]{2,1,0:T(2,128)(2,1)} %reshape.88), calls=%async_computation.1 | async-start | bytes 2097152 | tf_op jit(solution)/shard_map/all_to_all | solution.py:73
  97.8 1.7 copy-start.4
  122.9 34.8 %all-to-all-start.3 = ((bf16[64,2,4096]{2,1,0:T(2,128)(2,1)}), bf16[64,2,4096]{2,1,0:T(2,128)(2,1)S(1)}, u32[]{:S(2)}, u32[]{:S(2)}) async-start(bf16[64,2,4096]{2,1,0:T(2,128)(2,1)} %reshape.92), calls=%async_computation.3 | async-start | bytes 2097152 | tf_op jit(solution)/shard_map/all_to_all | solution.py:76
  131.0 144.0 %all-reduce.3.cloned.1.call-start = ((), (), s32[]{:S(2)}) async-start(), calls=%async_computation.4 | async-start | bytes 524288 | tf_op jit(solution)/shard_map/psum | solution.py:97
Sparse Core Ops, SparseCore 0:
  161.7 113.2 all-reduce.2

commit v2 on v1

v2 whole, which is shorter than its diff:
```python
import functools

import jax
import jax.numpy as jnp
from jax import lax
from jax.experimental import pallas as pl
from jax.experimental.pallas import tpu as pltpu
from jax.sharding import PartitionSpec as P

ROWS_Y = 8
CORES = 2
CAP = 2
LANE = 128
F32 = jnp.float32
BF16 = jnp.bfloat16
MESH = pl.DeviceIdType.MESH


def mm(a, b, ca=1, cb=0):
    return lax.dot_general(a, b, (((ca,), (cb,)), ((), ())), preferred_element_type=F32)


def when(cond, body):
    if cond is None:
        body()
    else:
        pl.when(cond)(body)


class Split:
    def __init__(self, n, tiles):
        self.n, self.tiles = n, tiles
        self.base, self.extra = tiles // n, tiles % n
        self.size = self.base + (1 if self.extra else 0)
        self.slots = 2 * self.size
        self.pieces = [(0, self.base, None)]
        if self.extra:
            self.pieces.append((self.base, 1, self.more_first))
        self.half = len(self.pieces)
        self.pieces.append((self.size, self.base, None))
        if self.extra:
            self.pieces.append((self.size + self.base, 1, self.more_second))

    def more_first(self, o):
        return o < self.extra

    def more_second(self, o):
        return o >= self.n - self.extra

    def first(self, o):
        return self.base * o + jnp.minimum(o, self.extra)

    def second(self, o):
        return self.base * o + jnp.maximum(o - (self.n - self.extra), 0)

    def static(self, o):
        a = self.base * o + min(o, self.extra)
        b = self.base * o + max(o - (self.n - self.extra), 0)
        na = self.base + (1 if o < self.extra else 0)
        nb = self.base + (1 if o >= self.n - self.extra and self.extra else 0)
        return [(j, 0, a + j) for j in range(na)] + [(self.size + j, 1, b + j) for j in range(nb)]


def iota(shape, axis):
    return lax.broadcasted_iota(jnp.int32, shape, axis)


def kernel(
    n, n_expert,
    route, codes, tokens, cot, wg, wu, wd,
    mixed, gtok, ggates, gdown,
    wgu, wdv, gdv, snd1, rcv1, snd2, gall, pre, ghid, part, hid, hidt, ggu,
    sndl, rcvl, sndr, rcvr, ybuf, rcv3, snd4, rcv4, fin, gfin,
    wsem, s1, r1, s2, r2, gs, gr, ls, lr, rs, rr, s3, r3, s4, r4, fs, fr, osem,
):
    ny = ROWS_Y
    a_n = n_expert // ny
    rows_y, rows_a = a_n * CAP, ny * CAP
    slots = n_expert * CAP
    top, tok_n = route.shape
    width = tokens.shape[1]
    tiles = width // LANE
    sp = Split(n, tiles)
    size, chunk_w = sp.size, sp.size * LANE
    r_max, l_max = n // 2, (n - 1) // 2

    z = lax.axis_index("dp")
    e = lax.axis_index("expert")
    core = lax.rem(e, CORES)
    y = lax.rem(e // CORES, ny)
    x = e // (CORES * ny)
    xc = x * CORES + core
    right, left = lax.rem(z + 1, n), lax.rem(z + n - 1, n)

    def y_peer(i):
        yp = lax.rem(y + i, ny)
        return yp, (z, (x * ny + yp) * CORES + core)

    def a_peer(i):
        ap = lax.rem(xc + i, a_n)
        return ap, (z, ((ap // CORES) * ny + y) * CORES + lax.rem(ap, CORES))

    def copy(src, dst, ssem, rsem, device):
        return pltpu.make_async_remote_copy(
            src_ref=src, dst_ref=dst, send_sem=ssem, recv_sem=rsem, device_id=device, device_id_type=MESH
        )

    f = wdv.shape[0]
    loads = [
        pltpu.make_async_copy(wg, wgu.at[pl.ds(0, width), pl.ds(0, f)], wsem.at[0]),
        pltpu.make_async_copy(wu, wgu.at[pl.ds(0, width), pl.ds(f, f)], wsem.at[1]),
        pltpu.make_async_copy(wd, wdv, wsem.at[2]),
    ]
    for load in loads:
        load.start()
    if sp.extra:
        wgu[pl.ds(width, LANE), :] = jnp.zeros((LANE, 2 * f), BF16)
        for o in range(n):
            held = {slot for slot, _, _ in sp.static(o)}
            for j in range(sp.slots):
                if j not in held:
                    gall[o, j] = jnp.zeros((slots, LANE), BF16)
    pre[...] = jnp.zeros_like(pre)
    ghid[...] = jnp.zeros_like(ghid)

    barrier = pltpu.get_barrier_semaphore()
    peers = [y_peer(i)[1] for i in range(1, ny)] + [a_peer(i)[1] for i in range(1, a_n)]
    peers += [(right, e), (left, e)]
    for peer in peers:
        pl.semaphore_signal(barrier, inc=1, device_id=peer, device_id_type=MESH)

    s_id = iota((slots, tok_n), 0)
    s_xc = (s_id // CAP) % a_n
    s_expert = ((s_xc // CORES) * ny + s_id // rows_y) * CORES + s_xc % CORES
    s_rank = (s_id % CAP).astype(F32)
    code_f = codes[...].astype(F32)
    gates = code_f / jnp.sum(code_f, axis=0, keepdims=True)
    hits = [route[k:k + 1, :] == s_expert for k in range(top)]
    named = jnp.zeros((slots, tok_n), F32)
    gate_of = jnp.zeros((slots, tok_n), F32)
    for k in range(top):
        named = named + jnp.where(hits[k], 1.0, 0.0)
        gate_of = gate_of + jnp.where(hits[k], gates[k:k + 1, :], 0.0)
    earlier = jnp.where(iota((tok_n, tok_n), 0) < iota((tok_n, tok_n), 1), 1.0, 0.0).astype(BF16)
    before = mm(named.astype(BF16), earlier)
    pick_f = jnp.where(before == s_rank, named, 0.0)
    pick = pick_f.astype(BF16)
    gate_of = gate_of * pick_f
    gate = jnp.sum(gate_of, axis=1, keepdims=True)

    def own_columns(ref, start, more):
        parts = []
        for j in range(size):
            at = jnp.minimum(start + j, tiles - 1)
            block = ref[:, pl.ds(pl.multiple_of(at * LANE, LANE), LANE)]
            if j >= sp.base:
                block = jnp.where(more(z), block, jnp.zeros_like(block))
            parts.append(block)
        return jnp.concatenate(parts, axis=1)

    def split_store(ref, slot0, value, groups):
        for j in range(value.shape[1] // LANE):
            ref[:, slot0 + j] = value[:, j * LANE:(j + 1) * LANE].reshape(groups, slots // groups, LANE)

    split_store(snd1, 0, mm(pick, own_columns(tokens, sp.first(z), sp.more_first)).astype(BF16), ny)
    cot_rows = mm(pick, own_columns(cot, sp.second(z), sp.more_second))
    split_store(snd1, size, (cot_rows * gate).astype(BF16), ny)

    pl.semaphore_wait(barrier, len(peers))

    def along_y(src, dst, ssem, rsem):
        copies = []
        for i in range(1, ny):
            yp, device = y_peer(i)
            copies.append(copy(src.at[yp], dst.at[y], ssem.at[i], rsem.at[i], device))
        for c in copies:
            c.start()
        dst[y] = src[y]
        for c in copies:
            c.wait_recv()
        return copies

    def regroup(src, outer, inner):
        to, at = iota((slots, slots), 0), iota((slots, slots), 1)
        want = ((to // CAP) % outer) * (inner * CAP) + (to // (outer * CAP)) * CAP + to % CAP
        move = jnp.where(at == want, 1.0, 0.0).astype(BF16)
        whole = jnp.concatenate([src[:, j].reshape(slots, LANE) for j in range(sp.slots)], axis=1)
        return mm(move, whole).astype(BF16)

    sends = along_y(snd1, rcv1, s1, r1)
    split_store(snd2, 0, regroup(rcv1, ny, a_n), a_n)
    copies = []
    rows = pl.ds(pl.multiple_of(xc * rows_a, rows_a), rows_a)
    for i in range(1, a_n):
        ap, device = a_peer(i)
        copies.append(copy(snd2.at[ap], gall.at[z, :, rows], s2.at[i], r2.at[i], device))
    for c in copies:
        c.start()
    for j in range(sp.slots):
        gall[z, j, rows] = snd2[xc, j]
    for c in copies:
        c.wait_recv()
    sends += copies

    def to_right(d):
        return lax.rem(z + n - d, n), (right, e)

    def to_left(d):
        return lax.rem(z + d, n), (left, e)

    ways = ((to_right, r_max), (to_left, l_max))

    def gather_copy(way, d, p):
        o, device = ways[way][0](d)
        at, count, cond = sp.pieces[p]
        block = gall.at[o, pl.ds(at, count)]
        return copy(block, block, gs.at[way, d, p], gr.at[way, d + 1, p], device), cond and cond(o)

    def gather_arrival(way, d, p):
        o, device = ways[way][0](d)
        at, count, cond = sp.pieces[p]
        block = gall.at[o, pl.ds(at, count)]
        return copy(block, block, gs.at[way, d, p], gr.at[way, d, p], device), cond and cond(o)

    def use_first(o):
        block = jnp.concatenate([gall[o, j] for j in range(size)], axis=1)
        at = pl.multiple_of(sp.first(o) * LANE, LANE)
        pre[...] += mm(block, wgu[pl.ds(at, chunk_w), :])

    def use_second(o):
        block = jnp.concatenate([gall[o, size + j] for j in range(size)], axis=1)
        at = pl.multiple_of(sp.second(o) * LANE, LANE)
        ghid[...] += mm(block, wdv[:, pl.ds(at, chunk_w)], 1, 1)

    def gather_step(d, forwards):
        for ps, use in ((range(sp.half), use_first), (range(sp.half, len(sp.pieces)), use_second)):
            for way in range(2):
                if forwards[way] is None:
                    continue
                for p in ps:
                    arrival, cond = gather_arrival(way, d, p)

                    def on(arrival=arrival, way=way, p=p):
                        arrival.wait_recv()
                        if forwards[way]:
                            gather_copy(way, d, p)[0].start()

                    when(cond, on)
            for way in range(2):
                if forwards[way] is not None:
                    use(ways[way][0](d)[0])

    for p in range(len(sp.pieces)):
        for way in range(2):
            c, cond = gather_copy(way, 0, p)
            when(cond, c.start)
    for load in loads:
        load.wait()
    use_first(z)
    use_second(z)

    def gather_body(d, carry):
        gather_step(d, (True, True))
        return carry

    lax.fori_loop(1, l_max, gather_body, 0)
    gather_step(l_max, (r_max > l_max, False))
    if r_max > l_max:
        gather_step(r_max, (False, None))

    gate_pre, up_pre, grad_hidden = pre[:, :f], pre[:, f:], ghid[...]
    sigma = 1.0 / (1.0 + jnp.exp(-gate_pre))
    silu = gate_pre * sigma
    hidden = silu * up_pre
    hid[...] = hidden.astype(BF16)
    hidt[...] = hidden.T.astype(BF16)
    ggu[:, :f] = (grad_hidden * up_pre * sigma * (1.0 + gate_pre * (1.0 - sigma))).astype(BF16)
    ggu[:, f:] = (grad_hidden * silu).astype(BF16)

    def make_part(which, o):
        at = pl.multiple_of(sp.first(o) * LANE, LANE)
        value = mm(ggu[...], wgu[pl.ds(at, chunk_w), :], 1, 1)
        for j in range(size):
            part[which, j] = value[:, j * LANE:(j + 1) * LANE]
        at = pl.multiple_of(sp.second(o) * LANE, LANE)
        value = mm(hid[...], wdv[:, pl.ds(at, chunk_w)])
        for j in range(size):
            part[which, size + j] = value[:, j * LANE:(j + 1) * LANE]

    flows = ((sndl, rcvl, ls, lr, to_right, (left, e)), (sndr, rcvr, rs, rr, to_left, (right, e)))

    def scatter_copy(flow, d, p):
        snd, rcv, ssem, rsem, owner, device = flows[flow]
        at, count, cond = sp.pieces[p]
        c = copy(snd.at[d, pl.ds(at, count)], rcv.at[d - 1, pl.ds(at, count)], ssem.at[d, p], rsem.at[d - 1, p], device)
        return c, cond and cond(owner(d)[0])

    def scatter_arrival(flow, d, p):
        snd, rcv, ssem, rsem, owner, device = flows[flow]
        at, count, cond = sp.pieces[p]
        c = copy(rcv.at[d, pl.ds(at, count)], rcv.at[d, pl.ds(at, count)], ssem.at[0, p], rsem.at[d, p], device)
        return c, cond and cond(owner(d)[0])

    def scatter_first(flow, d):
        snd = flows[flow][0]
        make_part(flow, flows[flow][4](d)[0])
        for p, (at, count, _) in enumerate(sp.pieces):
            c, cond = scatter_copy(flow, d, p)

            def on(c=c, at=at, count=count):
                snd[d, pl.ds(at, count)] = part[flow, pl.ds(at, count)].astype(BF16)
                c.start()

            when(cond, on)

    def scatter_step(flow_d):
        for flow, d in flow_d:
            make_part(flow, flows[flow][4](d)[0])
        for p, (at, count, _) in enumerate(sp.pieces):
            for flow, d in flow_d:
                snd, rcv = flows[flow][:2]
                arrival, cond = scatter_arrival(flow, d, p)

                def on(flow=flow, d=d, snd=snd, rcv=rcv, arrival=arrival):
                    arrival.wait_recv()
                    total = part[flow, pl.ds(at, count)] + rcv[d, pl.ds(at, count)].astype(F32)
                    snd[d, pl.ds(at, count)] = total.astype(BF16)
                    scatter_copy(flow, d, p)[0].start()

                when(cond, on)

    def make_gdown(o):
        block = jnp.concatenate([gall[o, size + j] for j in range(size)], axis=1)
        at = pl.multiple_of(sp.second(o) * LANE, LANE)
        gdv[:, pl.ds(at, chunk_w)] = mm(hidt[...], block).astype(BF16)

    scatter_first(0, r_max)
    scatter_first(1, l_max)

    def scatter_body(i, carry):
        scatter_step(((0, r_max - i), (1, l_max - i)))
        return carry

    lax.fori_loop(1, l_max, scatter_body, 0)
    if r_max > l_max:
        scatter_step(((0, 1),))

    def gdown_body(o, carry):
        make_gdown(o)
        return carry

    lax.fori_loop(0, n, gdown_body, 0)
    store = pltpu.make_async_copy(gdv, gdown, osem)
    store.start()

    make_part(0, z)
    for p, (at, count, _) in enumerate(sp.pieces):
        block = pl.ds(at, count)
        cond = None
        for flow in range(2):
            arrival, cond = scatter_arrival(flow, 0, p)
            when(cond, arrival.wait_recv)

        def on(block=block):
            total = part[0, block] + rcvl[0, block].astype(F32) + rcvr[0, block].astype(F32)
            ybuf[block] = total.astype(BF16)

        if cond is not None:
            ybuf[block] = jnp.zeros_like(ybuf[block])
        when(cond, on)

    copies = []
    for i in range(1, a_n):
        ap, device = a_peer(i)
        to = pl.ds(pl.multiple_of(ap * rows_a, rows_a), rows_a)
        copies.append(copy(ybuf.at[:, to], rcv3.at[xc], s3.at[i], r3.at[i], device))
    for c in copies:
        c.start()
    for j in range(sp.slots):
        rcv3[xc, j] = ybuf[j, rows]
    for c in copies:
        c.wait_recv()
    sends += copies
    split_store(snd4, 0, regroup(rcv3, a_n, ny), ny)
    sends += along_y(snd4, rcv4, s4, r4)

    back = [rcv4[:, j].reshape(slots, LANE) for j in range(sp.slots)]
    back_in, back_out = jnp.concatenate(back[:size], axis=1), jnp.concatenate(back[size:], axis=1)
    eye = jnp.where(iota((tok_n, tok_n), 0) == iota((tok_n, tok_n), 1), 1.0, 0.0).astype(BF16)
    high = gate_of.astype(BF16)
    low = (gate_of - high.astype(F32)).astype(BF16)
    high_t, low_t, pick_t = [mm(eye, v, 1, 1).astype(BF16) for v in (high, low, pick)]
    mixed_part = (mm(high_t, back_out) + mm(low_t, back_out)).astype(BF16)
    gtok_part = mm(pick_t, back_in).astype(BF16)
    for j in range(size):
        fin[z, j] = gtok_part[:, j * LANE:(j + 1) * LANE]
        fin[z, size + j] = mixed_part[:, j * LANE:(j + 1) * LANE]
    inner = mm(back_out, own_columns(cot, sp.second(z), sp.more_second), 1, 1) * pick_f
    gfin[z] = jnp.zeros(gfin.shape[1:], F32)
    for k in range(top):
        gfin[z, k:k + 1, 0:tok_n] = jnp.sum(jnp.where(hits[k], inner, 0.0), axis=0, keepdims=True)

    def final_copy(way, d, which, arrival):
        o, device = ways[way][0](d)
        ref = (fin, gfin)[which]
        return copy(ref.at[o], ref.at[o], fs.at[way, d, which], fr.at[way, d + (0 if arrival else 1), which], device)

    def final_step(d, forwards):
        for which in range(2):
            for way in range(2):
                if forwards[way] is None:
                    continue
                final_copy(way, d, which, True).wait_recv()
                if forwards[way]:
                    final_copy(way, d, which, False).start()

    for which in range(2):
        for way in range(2):
            final_copy(way, 0, which, False).start()

    def final_body(d, carry):
        final_step(d, (True, True))
        return carry

    lax.fori_loop(1, l_max, final_body, 0)
    final_step(l_max, (r_max > l_max, False))
    if r_max > l_max:
        final_step(r_max, (False, None))

    total = jnp.zeros(gfin.shape[1:], F32)
    for o in range(n):
        total = total + gfin[o]
        for slot, which, tile in sp.static(o):
            (gtok, mixed)[which][:, tile * LANE:(tile + 1) * LANE] = fin[o, slot]
    ggates[...] = total[:, 0:tok_n]

    for c in sends:
        c.wait_send()
    for way in range(2):

        def done(d, carry, way=way):
            for p in range(len(sp.pieces)):
                c, cond = gather_copy(way, d, p)
                when(cond, c.wait_send)
                c, cond = scatter_copy(way, d + 1, p)
                when(cond, c.wait_send)
            for which in range(2):
                final_copy(way, d, which, False).wait_send()
            return carry

        lax.fori_loop(0, (r_max, l_max)[way], done, 0)
    store.wait()


def local(n, n_expert, tokens, route, gate_code, cotangent, w_gate, w_up, w_down):
    tok_n, width = tokens.shape
    top = route.shape[1]
    f = w_gate.shape[2]
    ny, a_n = ROWS_Y, n_expert // ROWS_Y
    slots = n_expert * CAP
    sp = Split(n, width // LANE)
    k, np_ = sp.slots, len(sp.pieces)
    r_max, l_max = n // 2, (n - 1) // 2
    vmem = pl.BlockSpec(memory_space=pltpu.VMEM)
    anyw = pl.BlockSpec(memory_space=pl.ANY)
    dma = pltpu.SemaphoreType.DMA

    def b16(*shape):
        return pltpu.VMEM(shape, BF16)

    def f32(*shape):
        return pltpu.VMEM(shape, F32)

    rows_y, rows_a = a_n * CAP, ny * CAP
    mixed, gtok, ggates, gdown = pl.pallas_call(
        functools.partial(kernel, n, n_expert),
        out_shape=(
            jax.ShapeDtypeStruct((tok_n, width), BF16),
            jax.ShapeDtypeStruct((tok_n, width), BF16),
            jax.ShapeDtypeStruct((top, tok_n), F32),
            jax.ShapeDtypeStruct((f, width), BF16),
        ),
        in_specs=[vmem] * 4 + [anyw] * 3,
        out_specs=(vmem, vmem, vmem, anyw),
        scratch_shapes=[
            b16(width + (LANE if sp.extra else 0), 2 * f), b16(f, width), b16(f, width),
            b16(ny, k, rows_y, LANE), b16(ny, k, rows_y, LANE), b16(a_n, k, rows_a, LANE),
            b16(n, k, slots, LANE), f32(slots, 2 * f), f32(slots, f), f32(2, k, slots, LANE),
            b16(slots, f), b16(f, slots), b16(slots, 2 * f),
            b16(r_max + 1, k, slots, LANE), b16(r_max, k, slots, LANE),
            b16(l_max + 1, k, slots, LANE), b16(l_max, k, slots, LANE),
            b16(k, slots, LANE), b16(a_n, k, rows_a, LANE),
            b16(ny, k, rows_y, LANE), b16(ny, k, rows_y, LANE),
            b16(n, k, tok_n, LANE), f32(n, top, LANE),
            dma((3,)), dma((ny,)), dma((ny,)), dma((a_n,)), dma((a_n,)),
            dma((2, r_max, np_)), dma((2, r_max + 1, np_)),
            dma((r_max + 1, np_)), dma((r_max, np_)), dma((l_max + 1, np_)), dma((l_max, np_)),
            dma((a_n,)), dma((a_n,)), dma((ny,)), dma((ny,)),
            dma((2, r_max, 2)), dma((2, r_max + 1, 2)), dma,
        ],
        compiler_params=pltpu.CompilerParams(
            collective_id=0, has_side_effects=True, vmem_limit_bytes=48 * 1024 * 1024
        ),
        name="moe_step",
    )(route.T, gate_code.T, tokens, cotangent, w_gate[0], w_up[0], w_down[0])
    return mixed, gtok, ggates.T, gdown[None]


def solution(mesh):
    n, n_expert = mesh.shape["dp"], mesh.shape["expert"]
    return jax.shard_map(
        functools.partial(local, n, n_expert),
        mesh=mesh,
        in_specs=(
            P("expert", None),
            P("expert", None),
            P("expert", None),
            P("expert", None),
            P("expert", None, "dp"),
            P("expert", None, "dp"),
            P("expert", "dp", None),
        ),
        out_specs=(
            P("expert", None),
            P("expert", None),
            P("expert", None),
            P("expert", "dp", None),
        ),
        check_vma=False,
    )
```

time: 286 us -> 127 us (0.44)
  waiting for transfers between devices: 169 us -> 0 us
  Pallas kernels: 0 us -> 116 us
  starting transfers between devices: 38.6 us -> 0 us
  blocking collectives: 30.6 us -> 0 us
  between operations: 14.3 us -> 0.66 us
  matrix products: 13.4 us -> 0 us
  local copies, waits for them, and re-layouts: 18.4 us -> 9.04 us
    pallas_call x0 -> x1, Pallas kernels: none -> 116 us  [local(): pl.pallas_call(functools.partial(kernel, n, n_expert), out_shape=(jax.Sha...]
    all_to_all x4 -> x0, waiting for transfers between devices: 88.4 us -> none  [the longest x1 24.4 us: local(): lax.all_to_all(send_rows.reshape(shape3), 'expert', split_axis=0, concat_...]
    psum x1 -> x0, waiting for transfers between devices: 80.8 us -> none  [local(): lax.psum(mixed_part, 'dp')]
    all_to_all x4 -> x0, starting transfers between devices: 38.6 us -> none  [the longest x1 13.9 us: local(): lax.all_to_all(send_rows.reshape(shape3), 'expert', split_axis=0, concat_...]
    psum x1 -> x0, blocking collectives: 30.6 us -> none  [local(): lax.psum(gates_part, 'dp')]
    dot_general x11 -> x0, matrix products: 13.4 us -> none  [the longest x1 2.94 us: local(): lax.dot_general(placing, back_out.reshape(slot_count, width), (((0,), (0,...]
    reshape x9 -> x0, local copies, waits for them, and re-layouts: 12.5 us -> none  [the longest x1 2.25 us: local(): back_out.reshape(slot_count, width)]
    unnamed x18, local copies, waits for them, and re-layouts: 5.65 us -> 9.04 us
  transfers between devices with their start and end apart: 5 -> 0, of which waited for: 5 -> 0; matrix products, arithmetic and copies ran while one was open for 7% -> 0% of each run, Pallas kernels for 0% -> 0%
where the time goes in v2:
time: 127 us; the launch traced here: 126 us
  Pallas kernels  116 us (91%)
  local copies, waits for them, and re-layouts  9.04 us (7%)
    pallas_call x1, Pallas kernels, local(): pl.pallas_call(functools.partial(kernel, n, n_expert), out_shape=(jax.Sha...  116 us
    unnamed x18, local copies, waits for them, and re-layouts  9.04 us

profile of v2, /device:TPU:6, one launch (start us, length us, event | category | flops | bytes accessed | tf_op | source)
XLA Modules:
  0.0 126.1 jit_solution(16764604666033927812)
XLA Ops:
  0.6 0.0 copy-start.6
  0.6 0.0 copy-start.5
  0.7 0.7 copy-done.6
  1.3 0.0 copy-done.5
  1.3 0.0 copy-start
  1.3 1.2 copy-done
  2.6 0.0 copy-start.1
  2.6 1.2 copy-done.1
  3.8 0.0 copy-start.2
  3.8 1.2 copy-done.2
  5.0 0.0 copy-start.3
  5.0 0.9 copy-done.3
  5.9 0.0 copy-start.4
  5.9 0.9 copy-done.4
  6.8 116.4 %moe_step.1 = (bf16[16,4096]{1,0:T(8,128)(2,1)S(1)}, bf16[16,4096]{1,0:T(8,128)(2,1)S(1)}, f32[8,16]{1,0:T(8,128)S(1)}, bf16[128,4096]{1,0:T(8,128)(2,1)S(1)}) custom-call(s32[8,16]{1,0:T(8,128)S(1)} %bitcast.11, s32[8,16]{1,0:T(8,128)S(1)} %bitcast.12, bf16[16,4096]{1,0:T(8,128)(2,1)S(1)} %copy-done.3, bf16[16,4096]{1,0:T(8,128)(2,1)S(1)} %copy-done.4, ...), custom_call_target="tpu_custom_call" | custom-call | tf_op jit(solution)/shard_map/moe_step/pallas_call | solution.py:475
  123.2 0.7 copy.15
  123.9 0.7 copy.16
  124.6 0.6 copy.17
  125.1 1.0 copy.18
Async XLA Ops:
  0.6 0.7 copy-start.6
  0.6 0.7 copy-start.5
  1.3 1.2 copy-start
  2.6 1.2 copy-start.1
  3.8 1.2 copy-start.2
  5.0 0.9 copy-start.3
  5.9 0.9 copy-start.4

commit v3 on v2

v3 whole, which is shorter than its diff:
```python
import functools

import jax
import jax.numpy as jnp
from jax import lax
from jax.experimental import pallas as pl
from jax.experimental.pallas import tpu as pltpu
from jax.sharding import PartitionSpec as P

ROWS_Y = 8
CORES = 2
CAP = 2
LANE = 128
F32 = jnp.float32
BF16 = jnp.bfloat16
MESH = pl.DeviceIdType.MESH
DIRECT = 12
GROUPS = 2


def mm(a, b, ca=1, cb=0):
    return lax.dot_general(a, b, (((ca,), (cb,)), ((), ())), preferred_element_type=F32)


def when(cond, body):
    if cond is None:
        body()
    else:
        pl.when(cond)(body)


class Split:
    def __init__(self, n, tiles):
        self.n, self.tiles = n, tiles
        self.base, self.extra = tiles // n, tiles % n
        self.size = self.base + (1 if self.extra else 0)
        self.slots = 2 * self.size
        self.pieces = [(0, self.base, None)]
        if self.extra:
            self.pieces.append((self.base, 1, self.more_first))
        self.half = len(self.pieces)
        self.pieces.append((self.size, self.base, None))
        if self.extra:
            self.pieces.append((self.size + self.base, 1, self.more_second))

    def more_first(self, o):
        return o < self.extra

    def more_second(self, o):
        return o >= self.n - self.extra

    def first(self, o):
        return self.base * o + jnp.minimum(o, self.extra)

    def second(self, o):
        return self.base * o + jnp.maximum(o - (self.n - self.extra), 0)

    def group(self, p):
        return 0 if p < self.half else 1

    def static(self, o):
        a = self.base * o + min(o, self.extra)
        b = self.base * o + max(o - (self.n - self.extra), 0)
        na = self.base + (1 if o < self.extra else 0)
        nb = self.base + (1 if o >= self.n - self.extra and self.extra else 0)
        return [(j, 0, a + j) for j in range(na)] + [(self.size + j, 1, b + j) for j in range(nb)]


def iota(shape, axis):
    return lax.broadcasted_iota(jnp.int32, shape, axis)


def kernel(
    n, n_expert,
    route_h, codes_h, tokens_h, cot_h, wg, wu, wd,
    mixed, gtok, ggates, gdown,
    route, codes, tokens, cot, wgu, wdv, gdv, snd1, rcv1, snd2, gall, snd1d, rcv1d, snd2d, gdir, pre, ghid, part, hid, hidt, ggu,
    sndl, rcvl, sndr, rcvr, ybuf, snd3, rcv3, snd4, rcv4, fin, gfin,
    isem, wsem, s1, r1, s2, r2, s1d, r1d, s2d, r2d, gs, gr, ls, lr, rs, rr, s3, r3, s4, r4, fs, fr, osem,
):
    ny = ROWS_Y
    a_n = n_expert // ny
    rows_y, rows_a = a_n * CAP, ny * CAP
    slots = n_expert * CAP
    top, tok_n = route.shape
    width = tokens.shape[1]
    tiles = width // LANE
    direct = DIRECT if tiles > DIRECT else 0
    ringed = tiles - direct
    per = direct // GROUPS
    sd, sp = Split(n, ringed), Split(n, tiles)
    size, chunk_w = sp.size, sp.size * LANE
    hops = n // 2
    shared = n % 2 == 0

    def travels(hop, way, group):
        return hop < hops or (hop == hops and (not shared or way == group))

    z = lax.axis_index("dp")
    e = lax.axis_index("expert")
    core = lax.rem(e, CORES)
    y = lax.rem(e // CORES, ny)
    x = e // (CORES * ny)
    xc = x * CORES + core
    right, left = lax.rem(z + 1, n), lax.rem(z + n - 1, n)

    def y_peer(i):
        yp = lax.rem(y + i, ny)
        return yp, (z, (x * ny + yp) * CORES + core)

    def a_peer(i):
        ap = lax.rem(xc + i, a_n)
        return ap, (z, ((ap // CORES) * ny + y) * CORES + lax.rem(ap, CORES))

    def copy(src, dst, ssem, rsem, device):
        return pltpu.make_async_remote_copy(
            src_ref=src, dst_ref=dst, send_sem=ssem, recv_sem=rsem, device_id=device, device_id_type=MESH
        )

    for o in range(n):
        held = {slot for slot, _, _ in sd.static(o)}
        for j in range(sd.slots):
            if j not in held:
                gall[o, j] = jnp.zeros((slots, LANE), BF16)
    if sp.extra or sd.extra:
        wgu[pl.ds(width, LANE), :] = jnp.zeros((LANE, wgu.shape[1]), BF16)

    barrier = pltpu.get_barrier_semaphore()
    peers = [y_peer(i)[1] for i in range(1, ny)] + [a_peer(i)[1] for i in range(1, a_n)]
    peers += [(lax.rem(z + i, n), e) for i in range(1, n)]
    for peer in peers:
        pl.semaphore_signal(barrier, inc=1, device_id=peer, device_id_type=MESH)

    f = wdv.shape[0]
    inputs = [
        pltpu.make_async_copy(src, dst, isem.at[i])
        for i, (src, dst) in enumerate(((route_h, route), (codes_h, codes), (tokens_h, tokens), (cot_h, cot)))
    ]
    loads = [
        pltpu.make_async_copy(wg, wgu.at[pl.ds(0, width), pl.ds(0, f)], wsem.at[0]),
        pltpu.make_async_copy(wu, wgu.at[pl.ds(0, width), pl.ds(f, f)], wsem.at[1]),
        pltpu.make_async_copy(wd, wdv, wsem.at[2]),
    ]
    for load in inputs + loads:
        load.start()
    pre[...] = jnp.zeros_like(pre)
    ghid[...] = jnp.zeros_like(ghid)
    for load in inputs:
        load.wait()

    code_f = codes[...].astype(F32)
    gates = code_f / jnp.sum(code_f, axis=0, keepdims=True)
    earlier = jnp.where(iota((tok_n, tok_n), 0) < iota((tok_n, tok_n), 1), 1.0, 0.0).astype(BF16)

    def slots_of(s_y, s_xc):
        s_expert = ((s_xc // CORES) * ny + s_y) * CORES + s_xc % CORES
        hits = [route[k:k + 1, :] == s_expert for k in range(top)]
        named = jnp.zeros((slots, tok_n), F32)
        gate_of = jnp.zeros((slots, tok_n), F32)
        for k in range(top):
            named = named + jnp.where(hits[k], 1.0, 0.0)
            gate_of = gate_of + jnp.where(hits[k], gates[k:k + 1, :], 0.0)
        before = mm(named.astype(BF16), earlier)
        pick_f = jnp.where(before == (s_id % CAP).astype(F32), named, 0.0)
        gate_of = gate_of * pick_f
        return hits, pick_f, gate_of, jnp.sum(gate_of, axis=1, keepdims=True)

    s_id = iota((slots, tok_n), 0)
    hits, pick_f, gate_of, gate = by_y = slots_of(s_id // rows_y, (s_id // CAP) % a_n)
    pick = pick_f.astype(BF16)

    def own_columns(split, ref, start, more):
        parts = []
        for j in range(split.size):
            at = jnp.minimum(start + j, tiles - 1)
            block = ref[:, pl.ds(pl.multiple_of(at * LANE, LANE), LANE)]
            if j >= split.base:
                block = jnp.where(more(z), block, jnp.zeros_like(block))
            parts.append(block)
        return jnp.concatenate(parts, axis=1)

    def split_store(ref, slot0, value, groups):
        for j in range(value.shape[1] // LANE):
            ref[:, slot0 + j] = value[:, j * LANE:(j + 1) * LANE].reshape(groups, slots // groups, LANE)

    def pick_first(order, columns):
        return mm(order[1].astype(BF16), columns).astype(BF16)

    def pick_second(order, columns):
        return (mm(order[1].astype(BF16), columns) * order[3]).astype(BF16)

    split_store(snd1, 0, pick_first(by_y, own_columns(sd, tokens, sd.first(z), sd.more_first)), ny)
    split_store(snd1, sd.size, pick_second(by_y, own_columns(sd, cot, sd.second(z), sd.more_second)), ny)

    pl.semaphore_wait(barrier, len(peers))

    sends = []
    axes = {"y": (y_peer, ny, y), "a": (a_peer, a_n, xc)}

    def exchange(axis, src, dst, ssem, rsem, by_rows=False):
        peer, count, me = axes[axis]
        height = slots // count
        rows = pl.ds(pl.multiple_of(me * height, height), height)
        to = dst.at[:, rows] if by_rows else dst.at[me]
        copies = []
        for i in range(1, count):
            b, device = peer(i)
            copies.append(copy(src.at[b], to, ssem.at[i], rsem.at[i], device))
        for c in copies:
            c.start()
        if by_rows:
            for j in range(src.shape[1]):
                dst[j, rows] = src[me, j]
        else:
            dst[me] = src[me]
        sends.extend(copies)
        return copies

    def arrive(copies):
        for c in copies:
            c.wait_recv()

    def permute(whole, outer, inner):
        to, at = iota((slots, slots), 0), iota((slots, slots), 1)
        want = ((to // CAP) % outer) * (inner * CAP) + (to // (outer * CAP)) * CAP + to % CAP
        move = jnp.where(at == want, 1.0, 0.0).astype(BF16)
        return mm(move, whole).astype(BF16)

    def regroup(src, outer, inner):
        whole = jnp.concatenate([src[:, j].reshape(slots, LANE) for j in range(src.shape[1])], axis=1)
        return permute(whole, outer, inner)

    def build(g, order, groups):
        at = (ringed + g * per) * LANE
        split_store(snd1d.at[g], 0, pick_first(order, tokens[:, at:at + per * LANE]), groups)
        split_store(snd1d.at[g], per, pick_second(order, cot[:, at:at + per * LANE]), groups)

    own = exchange("y", snd1, rcv1, s1, r1)
    if direct:
        build(1, slots_of((s_id // CAP) % ny, s_id // rows_a), a_n)
        second = exchange("a", snd1d.at[1], rcv1d.at[1], s1d.at[1], r1d.at[1])
    arrive(own)
    split_store(snd2, 0, regroup(rcv1, ny, a_n), a_n)
    own = exchange("a", snd2, gall.at[z], s2, r2, True)
    if direct:
        build(0, by_y, ny)
        first = exchange("y", snd1d.at[0], rcv1d.at[0], s1d.at[0], r1d.at[0])
        arrive(second)
        split_store(snd2d.at[1], 0, regroup(rcv1d.at[1], a_n, ny), ny)
        second = exchange("y", snd2d.at[1], gdir.at[1], s2d.at[1], r2d.at[1], True)
    arrive(own)

    def first_turn():
        arrive(first)
        split_store(snd2d.at[0], 0, regroup(rcv1d.at[0], ny, a_n), a_n)
        return exchange("a", snd2d.at[0], gdir.at[0], s2d.at[0], r2d.at[0], True)

    def direct_use(g):
        at = (ringed + g * per) * LANE
        block = jnp.concatenate([gdir[g, j] for j in range(per)], axis=1)
        pre[...] += mm(block, wgu[at:at + per * LANE, :])
        block = jnp.concatenate([gdir[g, per + j] for j in range(per)], axis=1)
        ghid[...] += mm(block, wdv[:, at:at + per * LANE], 1, 1)

    def to_right(d):
        return lax.rem(z + n - d, n), (right, e)

    def to_left(d):
        return lax.rem(z + d, n), (left, e)

    ways = (to_right, to_left)

    def gather_copy(way, d, p, arrival=False):
        o, device = ways[way](d)
        at, count, cond = sd.pieces[p]
        block = gall.at[o, pl.ds(at, count)]
        to = d if arrival else d + 1
        return copy(block, block, gs.at[way, d, p], gr.at[way, to, p], device), cond and cond(o)

    def use_first(o):
        block = jnp.concatenate([gall[o, j] for j in range(sd.size)], axis=1)
        at = pl.multiple_of(sd.first(o) * LANE, LANE)
        pre[...] += mm(block, wgu[pl.ds(at, sd.size * LANE), :])

    def use_second(o):
        block = jnp.concatenate([gall[o, sd.size + j] for j in range(sd.size)], axis=1)
        at = pl.multiple_of(sd.second(o) * LANE, LANE)
        ghid[...] += mm(block, wdv[:, pl.ds(at, sd.size * LANE)], 1, 1)

    def gather_step(d):
        for group, use in ((0, use_first), (1, use_second)):
            for p in range(len(sd.pieces)):
                if sd.group(p) != group:
                    continue
                for way in range(2):
                    if not travels(d, way, group):
                        continue
                    came, cond = gather_copy(way, d, p, True)

                    def on(came=came, way=way, p=p, group=group):
                        came.wait_recv()
                        if travels(d + 1, way, group):
                            gather_copy(way, d, p)[0].start()

                    when(cond, on)
            for way in range(2):
                if travels(d, way, group):
                    use(ways[way](d)[0])

    for p in range(len(sd.pieces)):
        for way in range(2):
            if travels(1, way, sd.group(p)):
                c, cond = gather_copy(way, 0, p)
                when(cond, c.start)
    for load in loads:
        load.wait()
    use_first(z)
    use_second(z)
    for d in range(1, hops + 1):
        gather_step(d)
        if direct and d == max(1, hops - 3):
            first = first_turn()
    if direct:
        arrive(second)
        whole = jnp.concatenate([gdir[1, j] for j in range(2 * per)], axis=1)
        whole = permute(whole, ny, a_n)
        for j in range(2 * per):
            gdir[1, j] = whole[:, j * LANE:(j + 1) * LANE]
        direct_use(1)
        arrive(first)
        direct_use(0)

    gate_pre, up_pre, grad_hidden = pre[:, :f], pre[:, f:], ghid[...]
    sigma = 1.0 / (1.0 + jnp.exp(-gate_pre))
    silu = gate_pre * sigma
    hidden = silu * up_pre
    hid[...] = hidden.astype(BF16)
    hidt[...] = hidden.T.astype(BF16)
    ggu[:, :f] = (grad_hidden * up_pre * sigma * (1.0 + gate_pre * (1.0 - sigma))).astype(BF16)
    ggu[:, f:] = (grad_hidden * silu).astype(BF16)

    def make_part(which, o, group):
        if group == 0:
            at = pl.multiple_of(sp.first(o) * LANE, LANE)
            value = mm(ggu[...], wgu[pl.ds(at, chunk_w), :], 1, 1)
        else:
            at = pl.multiple_of(sp.second(o) * LANE, LANE)
            value = mm(hid[...], wdv[:, pl.ds(at, chunk_w)])
        for j in range(size):
            part[which, group * size + j] = value[:, j * LANE:(j + 1) * LANE]

    flows = ((sndl, rcvl, ls, lr, to_right, (left, e)), (sndr, rcvr, rs, rr, to_left, (right, e)))

    def scatter_copy(flow, d, p, arrival=False):
        snd, rcv, ssem, rsem, owner, device = flows[flow]
        at, count, cond = sp.pieces[p]
        to = d if arrival else d - 1
        c = copy(snd.at[d, pl.ds(at, count)], rcv.at[to, pl.ds(at, count)], ssem.at[d, p], rsem.at[to, p], device)
        return c, cond and cond(owner(d)[0])

    def scatter_step(d):
        for flow in range(2):
            for group in range(2):
                if travels(d, flow, group):
                    make_part(flow, flows[flow][4](d)[0], group)
        for p, (at, count, _) in enumerate(sp.pieces):
            for flow in range(2):
                if not travels(d, flow, sp.group(p)):
                    continue
                snd, rcv = flows[flow][:2]
                going, cond = scatter_copy(flow, d, p)

                def on(flow=flow, snd=snd, rcv=rcv, going=going, p=p, at=at, count=count):
                    total = part[flow, pl.ds(at, count)]
                    if travels(d + 1, flow, sp.group(p)):
                        scatter_copy(flow, d, p, True)[0].wait_recv()
                        total = total + rcv[d, pl.ds(at, count)].astype(F32)
                    snd[d, pl.ds(at, count)] = total.astype(BF16)
                    going.start()

                when(cond, on)

    def make_gdown(o):
        block = jnp.concatenate([gall[o, sd.size + j] for j in range(sd.size)], axis=1)
        at = pl.multiple_of(sd.second(o) * LANE, LANE)
        gdv[:, pl.ds(at, sd.size * LANE)] = mm(hidt[...], block).astype(BF16)

    done = 0
    for d in range(hops, 0, -1):
        scatter_step(d)
        while done < n * (hops - d + 1) // hops:
            make_gdown(done)
            done += 1
    for g in range(GROUPS if direct else 0):
        at = (ringed + g * per) * LANE
        block = jnp.concatenate([gdir[g, per + j] for j in range(per)], axis=1)
        gdv[:, at:at + per * LANE] = mm(hidt[...], block).astype(BF16)
    store = pltpu.make_async_copy(gdv, gdown, osem)
    store.start()

    make_part(0, z, 0)
    make_part(0, z, 1)
    for p, (at, count, _) in enumerate(sp.pieces):
        block = pl.ds(at, count)
        cond = None
        for flow in range(2):
            if travels(1, flow, sp.group(p)):
                came, cond = scatter_copy(flow, 0, p, True)
                when(cond, came.wait_recv)

        def on(block=block, p=p):
            total = part[0, block]
            for flow in range(2):
                if travels(1, flow, sp.group(p)):
                    total = total + flows[flow][1][0, block].astype(F32)
            ybuf[block] = total.astype(BF16)

        if cond is not None:
            ybuf[block] = jnp.zeros_like(ybuf[block])
        when(cond, on)

    for j in range(sp.slots):
        snd3[:, j] = ybuf[j].reshape(a_n, rows_a, LANE)
    arrive(exchange("a", snd3, rcv3, s3, r3))
    split_store(snd4, 0, regroup(rcv3, a_n, ny), ny)
    arrive(exchange("y", snd4, rcv4, s4, r4))

    back = [rcv4[:, j].reshape(slots, LANE) for j in range(sp.slots)]
    back_in, back_out = jnp.concatenate(back[:size], axis=1), jnp.concatenate(back[size:], axis=1)
    eye = jnp.where(iota((tok_n, tok_n), 0) == iota((tok_n, tok_n), 1), 1.0, 0.0).astype(BF16)
    high = gate_of.astype(BF16)
    low = (gate_of - high.astype(F32)).astype(BF16)
    high_t, low_t, pick_t = [mm(eye, v, 1, 1).astype(BF16) for v in (high, low, pick)]
    mixed_part = (mm(high_t, back_out) + mm(low_t, back_out)).astype(BF16)
    gtok_part = mm(pick_t, back_in).astype(BF16)
    shift = 1 if sp.extra else 0

    def place(slot):
        if slot < size:
            return 0 if slot >= sp.base else slot + shift
        return slot - size + sp.base + shift

    for j in range(size):
        fin[z, place(j)] = gtok_part[:, j * LANE:(j + 1) * LANE]
        fin[z, place(size + j)] = mixed_part[:, j * LANE:(j + 1) * LANE]
    inner = mm(back_out, own_columns(sp, cot, sp.second(z), sp.more_second), 1, 1) * pick_f
    inner = jnp.concatenate(
        [jnp.sum(jnp.where(hits[k], inner, 0.0), axis=0, keepdims=True) for k in range(top)], axis=0
    )
    lane, line = iota((tok_n, LANE), 1), iota((tok_n, LANE), 0)
    spread = jnp.where((lane % tok_n == line) & (lane < top * tok_n), 1.0, 0.0)
    mine = iota((top, LANE), 1) // tok_n == iota((top, LANE), 0)

    def exact(a, b, cb):
        return lax.dot_general(
            a, b, (((1,), (cb,)), ((), ())), precision=lax.Precision.HIGHEST, preferred_element_type=F32
        )

    gfin[z] = jnp.sum(jnp.where(mine, exact(inner, spread, 0), 0.0), axis=0, keepdims=True)

    kinds = ((False, False), (True, False), (False, True), (True, True))

    def ranges(o):
        if not sp.extra:
            return [(0, sp.slots, None)]
        out = []
        for first, second in kinds:
            a, b = sp.more_first(o), sp.more_second(o)
            cond = (a if first else jnp.logical_not(a)) & (b if second else jnp.logical_not(b))
            at = 0 if first else 1
            out.append((at, 2 * sp.base + 1 - at + (1 if second else 0), cond))
        return out

    def final_copies(i, o, device):
        out = [(copy(fin.at[o, pl.ds(at, count)], fin.at[o, pl.ds(at, count)], fs.at[i, 0], fr.at[i, 0], device), cond)
               for at, count, cond in ranges(o)]
        out.append((copy(gfin.at[o], gfin.at[o], fs.at[i, 1], fr.at[i, 1], device), None))
        return out

    finals = [final_copies(i, z, (lax.rem(z + i, n), e)) for i in range(1, n)]
    for i in sorted(range(1, n), key=lambda i: -min(i, n - i)):
        for c, cond in finals[i - 1]:
            when(cond, c.start)
    for i in range(1, n):
        for c, cond in final_copies(i, lax.rem(z + n - i, n), (right, e)):
            when(cond, c.wait_recv)

    total = jnp.zeros(gfin.shape[1:], F32)
    for o in range(n):
        total = total + gfin[o]
        for slot, which, tile in sp.static(o):
            (gtok, mixed)[which][:, tile * LANE:(tile + 1) * LANE] = fin[o, place(slot)]
    ggates[...] = exact(jnp.where(mine, total, 0.0), spread, 1)

    for c in sends:
        c.wait_send()
    for way in range(2):

        def left_at(d, carry, way=way):
            for split, pieces_copy, first in ((sd, gather_copy, 0), (sp, scatter_copy, 1)):
                for p in range(len(split.pieces)):
                    if travels(d + 1, way, split.group(p)):
                        c, cond = pieces_copy(way, d + first, p)
                        when(cond, c.wait_send)
            return carry

        for d in range(hops):
            left_at(d, 0)
    for copies in finals:
        for c, cond in copies:
            when(cond, c.wait_send)
    store.wait()


def local(n, n_expert, tokens, route, gate_code, cotangent, w_gate, w_up, w_down):
    tok_n, width = tokens.shape
    top = route.shape[1]
    f = w_gate.shape[2]
    ny, a_n = ROWS_Y, n_expert // ROWS_Y
    slots = n_expert * CAP
    tiles = width // LANE
    direct = DIRECT if tiles > DIRECT else 0
    sd, sp = Split(n, tiles - direct), Split(n, tiles)
    k, np_ = sp.slots, len(sp.pieces)
    kd, npd = sd.slots, len(sd.pieces)
    groups, per2 = (GROUPS, 2 * direct // GROUPS) if direct else (1, 1)
    hops = n // 2
    vmem = pl.BlockSpec(memory_space=pltpu.VMEM)
    anyw = pl.BlockSpec(memory_space=pl.ANY)
    dma = pltpu.SemaphoreType.DMA

    def b16(*shape):
        return pltpu.VMEM(shape, BF16)

    def f32(*shape):
        return pltpu.VMEM(shape, F32)

    rows_y, rows_a = a_n * CAP, ny * CAP
    mixed, gtok, ggates, gdown = pl.pallas_call(
        functools.partial(kernel, n, n_expert),
        out_shape=(
            jax.ShapeDtypeStruct((tok_n, width), BF16),
            jax.ShapeDtypeStruct((tok_n, width), BF16),
            jax.ShapeDtypeStruct((top, tok_n), F32),
            jax.ShapeDtypeStruct((f, width), BF16),
        ),
        in_specs=[anyw] * 7,
        out_specs=(vmem, vmem, vmem, anyw),
        scratch_shapes=[
            pltpu.VMEM((top, tok_n), jnp.int32), pltpu.VMEM((top, tok_n), jnp.int32),
            b16(tok_n, width), b16(tok_n, width),
            b16(width + LANE, 2 * f), b16(f, width), b16(f, width),
            b16(ny, kd, rows_y, LANE), b16(ny, kd, rows_y, LANE), b16(a_n, kd, rows_a, LANE),
            b16(n, kd, slots, LANE),
            b16(groups, ny, per2, rows_y, LANE), b16(groups, ny, per2, rows_y, LANE),
            b16(groups, a_n, per2, rows_a, LANE), b16(groups, per2, slots, LANE),
            f32(slots, 2 * f), f32(slots, f), f32(2, k, slots, LANE),
            b16(slots, f), b16(f, slots), b16(slots, 2 * f),
            b16(hops + 1, k, slots, LANE), b16(hops, k, slots, LANE),
            b16(hops + 1, k, slots, LANE), b16(hops, k, slots, LANE),
            b16(k, slots, LANE), b16(a_n, k, rows_a, LANE), b16(a_n, k, rows_a, LANE),
            b16(ny, k, rows_y, LANE), b16(ny, k, rows_y, LANE),
            b16(n, k, tok_n, LANE), f32(n, 1, LANE),
            dma((4,)), dma((3,)), dma((ny,)), dma((ny,)), dma((a_n,)), dma((a_n,)),
            dma((groups, ny)), dma((groups, ny)), dma((groups, a_n)), dma((groups, a_n)),
            dma((2, hops, npd)), dma((2, hops + 1, npd)),
            dma((hops + 1, np_)), dma((hops, np_)), dma((hops + 1, np_)), dma((hops, np_)),
            dma((a_n,)), dma((a_n,)), dma((ny,)), dma((ny,)),
            dma((n, 2)), dma((n, 2)), dma,
        ],
        compiler_params=pltpu.CompilerParams(
            collective_id=0, has_side_effects=True, vmem_limit_bytes=60 * 1024 * 1024
        ),
        name="moe_step",
    )(route.T, gate_code.T, tokens, cotangent, w_gate[0], w_up[0], w_down[0])
    return mixed, gtok, ggates.T, gdown[None]


def solution(mesh):
    n, n_expert = mesh.shape["dp"], mesh.shape["expert"]
    return jax.shard_map(
        functools.partial(local, n, n_expert),
        mesh=mesh,
        in_specs=(
            P("expert", None),
            P("expert", None),
            P("expert", None),
            P("expert", None),
            P("expert", None, "dp"),
            P("expert", None, "dp"),
            P("expert", "dp", None),
        ),
        out_specs=(
            P("expert", None),
            P("expert", None),
            P("expert", None),
            P("expert", "dp", None),
        ),
        check_vma=False,
    )
```

time: 127 us -> 110 us (0.87)
  Pallas kernels: 116 us -> 103 us
  local copies, waits for them, and re-layouts: 9.04 us -> 5.17 us
    pallas_call x1, Pallas kernels: 116 us -> 103 us  [local(): pl.pallas_call(functools.partial(kernel, n, n_expert), out_shape=(jax.Sha...]
    unnamed x18 -> x8, local copies, waits for them, and re-layouts: 9.04 us -> 5.17 us
where the time goes in v3:
time: 110 us; the launch traced here: 109 us
  Pallas kernels  103 us (94%)
  local copies, waits for them, and re-layouts  5.17 us (5%)
    pallas_call x1, Pallas kernels, local(): pl.pallas_call(functools.partial(kernel, n, n_expert), out_shape=(jax.Sha...  103 us
    unnamed x8, local copies, waits for them, and re-layouts  5.17 us

profile of v3, /device:TPU:6, one launch (start us, length us, event | category | flops | bytes accessed | tf_op | source)
XLA Modules:
  0.0 109.2 jit_solution(6803505951262331900)
XLA Ops:
  0.6 103.3 %moe_step.1 = (bf16[16,4096]{1,0:T(8,128)(2,1)}, bf16[16,4096]{1,0:T(8,128)(2,1)}, f32[8,16]{1,0:T(8,128)}, bf16[128,4096]{1,0:T(8,128)(2,1)}) custom-call(s32[8,16]{1,0:T(8,128)} %bitcast.11, s32[8,16]{1,0:T(8,128)} %bitcast.12, bf16[16,4096]{1,0:T(8,128)(2,1)} %tokens_h.1, bf16[16,4096]{1,0:T(8,128)(2,1)} %cot_h.1, bf16[4096,128]{1,0:T(8,128)(2,1)} %bitcast.7, ...), custom_call_target="tpu_custom_call" | custom-call | tf_op jit(solution)/shard_map/moe_step/pallas_call | solution.py:539
  104.0 0.0 copy-start
  104.0 1.6 %copy.15 = bf16[16,4096]{1,0:T(8,128)(2,1)} copy(bf16[16,4096]{1,0:T(8,128)(2,1)} %get-tuple-element.16) | data formatting | bytes 262144
  105.6 0.0 copy-done
  105.6 0.0 copy-start.1
  105.6 0.7 copy.16
  106.3 0.0 copy-done.1
  106.3 0.6 copy.17
  106.9 2.3 %copy.18 = bf16[1,128,4096]{2,1,0:T(8,128)(2,1)} copy(bf16[1,128,4096]{2,1,0:T(8,128)(2,1)} %bitcast.10) | data formatting | bytes 2097152
Async XLA Ops:
  104.0 1.6 %copy-start = (bf16[16,4096]{1,0:T(8,128)(2,1)S(1)}, bf16[16,4096]{1,0:T(8,128)(2,1)}, u32[]{:S(2)}) copy-start(bf16[16,4096]{1,0:T(8,128)(2,1)} %get-tuple-element.17) | copy-start | bytes 393220
  105.6 0.7 copy-start.1

commit v4 on v3

--- a/solution.py
+++ b/solution.py
@@ -14,8 +14,8 @@
 F32 = jnp.float32
 BF16 = jnp.bfloat16
 MESH = pl.DeviceIdType.MESH
-DIRECT = 12
-GROUPS = 2
+DIRECT = (4, 4)
+TURN = 1
 
 
 def mm(a, b, ca=1, cb=0):
@@ -35,11 +35,11 @@
         self.base, self.extra = tiles // n, tiles % n
         self.size = self.base + (1 if self.extra else 0)
         self.slots = 2 * self.size
-        self.pieces = [(0, self.base, None)]
+        self.pieces = [(j, 1, None) for j in range(self.base)]
         if self.extra:
             self.pieces.append((self.base, 1, self.more_first))
         self.half = len(self.pieces)
-        self.pieces.append((self.size, self.base, None))
+        self.pieces += [(self.size + j, 1, None) for j in range(self.base)]
         if self.extra:
             self.pieces.append((self.size + self.base, 1, self.more_second))
 
@@ -75,8 +75,8 @@
     route_h, codes_h, tokens_h, cot_h, wg, wu, wd,
     mixed, gtok, ggates, gdown,
     route, codes, tokens, cot, wgu, wdv, gdv, snd1, rcv1, snd2, gall, snd1d, rcv1d, snd2d, gdir, pre, ghid, part, hid, hidt, ggu,
-    sndl, rcvl, sndr, rcvr, ybuf, snd3, rcv3, snd4, rcv4, fin, gfin,
-    isem, wsem, s1, r1, s2, r2, s1d, r1d, s2d, r2d, gs, gr, ls, lr, rs, rr, s3, r3, s4, r4, fs, fr, osem,
+    sndl, rcvl, sndr, rcvr, ybuf, snd3, rcv3, snd4, rcv4, snd5, rcv5, snd6, rcv6, zsnd, zrcv, fin, gfin,
+    isem, wsem, s1, r1, s2, r2, s1d, r1d, s2d, r2d, gs, gr, ls, lr, rs, rr, s3, r3, s4, r4, fs, fr, osem, s5, r5, s6, r6, zs, zr,
 ):
     ny = ROWS_Y
     a_n = n_expert // ny
@@ -85,16 +85,22 @@
     top, tok_n = route.shape
     width = tokens.shape[1]
     tiles = width // LANE
-    direct = DIRECT if tiles > DIRECT else 0
-    ringed = tiles - direct
-    per = direct // GROUPS
-    sd, sp = Split(n, ringed), Split(n, tiles)
-    size, chunk_w = sp.size, sp.size * LANE
-    hops = n // 2
-    shared = n % 2 == 0
+    direct = DIRECT if tiles > sum(DIRECT) else ()
+    ringed = tiles - sum(direct)
+    m = n // 2 if n % 2 == 0 else n
+    sd, sp = Split(m, ringed), Split(n, tiles)
+    late = sp.extra
+    kept = tiles - late
+    per_b = late // 2
+    sb = Split(n, kept)
+    size, chunk_w = sb.size, sb.size * LANE
+    hops, hops_in = n // 2, m // 2
 
     def travels(hop, way, group):
-        return hop < hops or (hop == hops and (not shared or way == group))
+        return hop < hops or (hop == hops and (n % 2 == 1 or way == group))
+
+    def travels_in(hop, way, group):
+        return hop < hops_in or (hop == hops_in and (m % 2 == 1 or way == group))
 
     z = lax.axis_index("dp")
     e = lax.axis_index("expert")
@@ -103,6 +109,7 @@
     x = e // (CORES * ny)
     xc = x * CORES + core
     right, left = lax.rem(z + 1, n), lax.rem(z + n - 1, n)
+    zm = lax.rem(z, m)
 
     def y_peer(i):
         yp = lax.rem(y + i, ny)
@@ -117,7 +124,7 @@
             src_ref=src, dst_ref=dst, send_sem=ssem, recv_sem=rsem, device_id=device, device_id_type=MESH
         )
 
-    for o in range(n):
+    for o in range(m):
         held = {slot for slot, _, _ in sd.static(o)}
         for j in range(sd.slots):
             if j not in held:
@@ -166,16 +173,17 @@
         return hits, pick_f, gate_of, jnp.sum(gate_of, axis=1, keepdims=True)
 
     s_id = iota((slots, tok_n), 0)
-    hits, pick_f, gate_of, gate = by_y = slots_of(s_id // rows_y, (s_id // CAP) % a_n)
-    pick = pick_f.astype(BF16)
-
-    def own_columns(split, ref, start, more):
+    by_y = slots_of(s_id // rows_y, (s_id // CAP) % a_n)
+    by_a = slots_of((s_id // CAP) % ny, s_id // rows_a)
+
+    def own_columns(split, ref, which, o):
+        start, more = ((split.first, split.more_first), (split.second, split.more_second))[which]
         parts = []
         for j in range(split.size):
-            at = jnp.minimum(start + j, tiles - 1)
+            at = jnp.minimum(start(o) + j, tiles - 1)
             block = ref[:, pl.ds(pl.multiple_of(at * LANE, LANE), LANE)]
             if j >= split.base:
-                block = jnp.where(more(z), block, jnp.zeros_like(block))
+                block = jnp.where(more(o), block, jnp.zeros_like(block))
             parts.append(block)
         return jnp.concatenate(parts, axis=1)
 
@@ -189,8 +197,8 @@
     def pick_second(order, columns):
         return (mm(order[1].astype(BF16), columns) * order[3]).astype(BF16)
 
-    split_store(snd1, 0, pick_first(by_y, own_columns(sd, tokens, sd.first(z), sd.more_first)), ny)
-    split_store(snd1, sd.size, pick_second(by_y, own_columns(sd, cot, sd.second(z), sd.more_second)), ny)
+    split_store(snd1, 0, pick_first(by_y, own_columns(sd, tokens, 0, zm)), ny)
+    split_store(snd1, sd.size, pick_second(by_y, own_columns(sd, cot, 1, zm)), ny)
 
     pl.semaphore_wait(barrier, len(peers))
 
@@ -230,37 +238,48 @@
         whole = jnp.concatenate([src[:, j].reshape(slots, LANE) for j in range(src.shape[1])], axis=1)
         return permute(whole, outer, inner)
 
+    def columns_of(g):
+        at = (ringed + sum(direct[:g])) * LANE
+        return slice(at, at + direct[g] * LANE)
+
+    def tiles_of(ref, g):
+        return ref.at[g, :, pl.ds(0, 2 * direct[g])]
+
     def build(g, order, groups):
-        at = (ringed + g * per) * LANE
-        split_store(snd1d.at[g], 0, pick_first(order, tokens[:, at:at + per * LANE]), groups)
-        split_store(snd1d.at[g], per, pick_second(order, cot[:, at:at + per * LANE]), groups)
+        split_store(tiles_of(snd1d, g), 0, pick_first(order, tokens[:, columns_of(g)]), groups)
+        split_store(tiles_of(snd1d, g), direct[g], pick_second(order, cot[:, columns_of(g)]), groups)
+
+    def direct_out(g, axis):
+        return exchange(axis, tiles_of(snd1d, g), tiles_of(rcv1d, g), s1d.at[g], r1d.at[g])
+
+    def direct_on(g, axis, outer, inner):
+        split_store(snd2d.at[g], 0, regroup(tiles_of(rcv1d, g), outer, inner), inner)
+        to = gdir.at[g, pl.ds(0, 2 * direct[g])]
+        return exchange(axis, tiles_of(snd2d, g), to, s2d.at[g], r2d.at[g], True)
 
     own = exchange("y", snd1, rcv1, s1, r1)
     if direct:
-        build(1, slots_of((s_id // CAP) % ny, s_id // rows_a), a_n)
-        second = exchange("a", snd1d.at[1], rcv1d.at[1], s1d.at[1], r1d.at[1])
+        build(1, by_a, a_n)
+        second = direct_out(1, "a")
     arrive(own)
     split_store(snd2, 0, regroup(rcv1, ny, a_n), a_n)
-    own = exchange("a", snd2, gall.at[z], s2, r2, True)
+    own = exchange("a", snd2, gall.at[zm], s2, r2, True)
     if direct:
         build(0, by_y, ny)
-        first = exchange("y", snd1d.at[0], rcv1d.at[0], s1d.at[0], r1d.at[0])
+        first = direct_out(0, "y")
         arrive(second)
-        split_store(snd2d.at[1], 0, regroup(rcv1d.at[1], a_n, ny), ny)
-        second = exchange("y", snd2d.at[1], gdir.at[1], s2d.at[1], r2d.at[1], True)
+        second = direct_on(1, "y", a_n, ny)
     arrive(own)
 
     def first_turn():
         arrive(first)
-        split_store(snd2d.at[0], 0, regroup(rcv1d.at[0], ny, a_n), a_n)
-        return exchange("a", snd2d.at[0], gdir.at[0], s2d.at[0], r2d.at[0], True)
+        return direct_on(0, "a", ny, a_n)
 
     def direct_use(g):
-        at = (ringed + g * per) * LANE
-        block = jnp.concatenate([gdir[g, j] for j in range(per)], axis=1)
-        pre[...] += mm(block, wgu[at:at + per * LANE, :])
-        block = jnp.concatenate([gdir[g, per + j] for j in range(per)], axis=1)
-        ghid[...] += mm(block, wdv[:, at:at + per * LANE], 1, 1)
+        block = jnp.concatenate([gdir[g, j] for j in range(direct[g])], axis=1)
+        pre[...] += mm(block, wgu[columns_of(g), :])
+        block = jnp.concatenate([gdir[g, direct[g] + j] for j in range(direct[g])], axis=1)
+        ghid[...] += mm(block, wdv[:, columns_of(g)], 1, 1)
 
     def to_right(d):
         return lax.rem(z + n - d, n), (right, e)
@@ -272,6 +291,7 @@
 
     def gather_copy(way, d, p, arrival=False):
         o, device = ways[way](d)
+        o = lax.rem(o, m)
         at, count, cond = sd.pieces[p]
         block = gall.at[o, pl.ds(at, count)]
         to = d if arrival else d + 1
@@ -293,38 +313,38 @@
                 if sd.group(p) != group:
                     continue
                 for way in range(2):
-                    if not travels(d, way, group):
+                    if not travels_in(d, way, group):
                         continue
                     came, cond = gather_copy(way, d, p, True)
 
                     def on(came=came, way=way, p=p, group=group):
                         came.wait_recv()
-                        if travels(d + 1, way, group):
+                        if travels_in(d + 1, way, group):
                             gather_copy(way, d, p)[0].start()
 
                     when(cond, on)
             for way in range(2):
-                if travels(d, way, group):
-                    use(ways[way](d)[0])
+                if travels_in(d, way, group):
+                    use(lax.rem(ways[way](d)[0], m))
 
     for p in range(len(sd.pieces)):
         for way in range(2):
-            if travels(1, way, sd.group(p)):
+            if travels_in(1, way, sd.group(p)):
                 c, cond = gather_copy(way, 0, p)
                 when(cond, c.start)
     for load in loads:
         load.wait()
-    use_first(z)
-    use_second(z)
-    for d in range(1, hops + 1):
+    use_first(zm)
+    use_second(zm)
+    for d in range(1, hops_in + 1):
         gather_step(d)
-        if direct and d == max(1, hops - 3):
+        if direct and d == TURN:
             first = first_turn()
     if direct:
         arrive(second)
-        whole = jnp.concatenate([gdir[1, j] for j in range(2 * per)], axis=1)
+        whole = jnp.concatenate([gdir[1, j] for j in range(2 * direct[1])], axis=1)
         whole = permute(whole, ny, a_n)
-        for j in range(2 * per):
+        for j in range(2 * direct[1]):
             gdir[1, j] = whole[:, j * LANE:(j + 1) * LANE]
         direct_use(1)
         arrive(first)
@@ -341,10 +361,10 @@
 
     def make_part(which, o, group):
         if group == 0:
-            at = pl.multiple_of(sp.first(o) * LANE, LANE)
+            at = pl.multiple_of(sb.first(o) * LANE, LANE)
             value = mm(ggu[...], wgu[pl.ds(at, chunk_w), :], 1, 1)
         else:
-            at = pl.multiple_of(sp.second(o) * LANE, LANE)
+            at = pl.multiple_of(sb.second(o) * LANE, LANE)
             value = mm(hid[...], wdv[:, pl.ds(at, chunk_w)])
         for j in range(size):
             part[which, group * size + j] = value[:, j * LANE:(j + 1) * LANE]
@@ -353,7 +373,7 @@
 
     def scatter_copy(flow, d, p, arrival=False):
         snd, rcv, ssem, rsem, owner, device = flows[flow]
-        at, count, cond = sp.pieces[p]
+        at, count, cond = sb.pieces[p]
         to = d if arrival else d - 1
         c = copy(snd.at[d, pl.ds(at, count)], rcv.at[to, pl.ds(at, count)], ssem.at[d, p], rsem.at[to, p], device)
         return c, cond and cond(owner(d)[0])
@@ -363,16 +383,16 @@
             for group in range(2):
                 if travels(d, flow, group):
                     make_part(flow, flows[flow][4](d)[0], group)
-        for p, (at, count, _) in enumerate(sp.pieces):
+        for p, (at, count, _) in enumerate(sb.pieces):
             for flow in range(2):
-                if not travels(d, flow, sp.group(p)):
+                if not travels(d, flow, sb.group(p)):
                     continue
                 snd, rcv = flows[flow][:2]
                 going, cond = scatter_copy(flow, d, p)
 
                 def on(flow=flow, snd=snd, rcv=rcv, going=going, p=p, at=at, count=count):
                     total = part[flow, pl.ds(at, count)]
-                    if travels(d + 1, flow, sp.group(p)):
+                    if travels(d + 1, flow, sb.group(p)):
                         scatter_copy(flow, d, p, True)[0].wait_recv()
                         total = total + rcv[d, pl.ds(at, count)].astype(F32)
                     snd[d, pl.ds(at, count)] = total.astype(BF16)
@@ -385,33 +405,55 @@
         at = pl.multiple_of(sd.second(o) * LANE, LANE)
         gdv[:, pl.ds(at, sd.size * LANE)] = mm(hidt[...], block).astype(BF16)
 
+    back_first = []
+
+    def back_start():
+        for g in range(2):
+            cols = pl.ds((kept + g * per_b) * LANE, per_b * LANE)
+            whole = jnp.concatenate([mm(ggu[...], wgu[cols, :], 1, 1), mm(hid[...], wdv[:, cols])], axis=1).astype(BF16)
+            if g == 1:
+                whole = permute(whole, a_n, ny)
+            split_store(snd5.at[g], 0, whole, (a_n, ny)[g])
+            back_first.append(exchange("ay"[g], snd5.at[g], rcv5.at[g], s5.at[g], r5.at[g]))
+
+    def back_turn(g):
+        arrive(back_first[g])
+        outer, inner = ((a_n, ny), (ny, a_n))[g]
+        split_store(snd6.at[g], 0, regroup(rcv5.at[g], outer, inner), inner)
+        return exchange("ya"[g], snd6.at[g], rcv6.at[g], s6.at[g], r6.at[g])
+
     done = 0
     for d in range(hops, 0, -1):
         scatter_step(d)
-        while done < n * (hops - d + 1) // hops:
+        if late and d == hops:
+            back_start()
+        if late and d == max(1, hops - 2):
+            back = [back_turn(0)]
+        if late and d == max(1, hops - 4):
+            back.append(back_turn(1))
+        while done < m * (hops - d + 1) // hops:
             make_gdown(done)
             done += 1
-    for g in range(GROUPS if direct else 0):
-        at = (ringed + g * per) * LANE
-        block = jnp.concatenate([gdir[g, per + j] for j in range(per)], axis=1)
-        gdv[:, at:at + per * LANE] = mm(hidt[...], block).astype(BF16)
+    for g in range(len(direct)):
+        block = jnp.concatenate([gdir[g, direct[g] + j] for j in range(direct[g])], axis=1)
+        gdv[:, columns_of(g)] = mm(hidt[...], block).astype(BF16)
     store = pltpu.make_async_copy(gdv, gdown, osem)
     store.start()
 
     make_part(0, z, 0)
     make_part(0, z, 1)
-    for p, (at, count, _) in enumerate(sp.pieces):
+    for p, (at, count, _) in enumerate(sb.pieces):
         block = pl.ds(at, count)
         cond = None
         for flow in range(2):
-            if travels(1, flow, sp.group(p)):
+            if travels(1, flow, sb.group(p)):
                 came, cond = scatter_copy(flow, 0, p, True)
                 when(cond, came.wait_recv)
 
         def on(block=block, p=p):
             total = part[0, block]
             for flow in range(2):
-                if travels(1, flow, sp.group(p)):
+                if travels(1, flow, sb.group(p)):
                     total = total + flows[flow][1][0, block].astype(F32)
             ybuf[block] = total.astype(BF16)
 
@@ -419,34 +461,74 @@
             ybuf[block] = jnp.zeros_like(ybuf[block])
         when(cond, on)
 
-    for j in range(sp.slots):
+    def at_home(order, back_in, back_out, cot_columns):
+        hits, pick_f, gate_of = order[:3]
+        high = gate_of.astype(BF16)
+        low = (gate_of - high.astype(F32)).astype(BF16)
+        eye = jnp.where(iota((tok_n, tok_n), 0) == iota((tok_n, tok_n), 1), 1.0, 0.0).astype(BF16)
+        high_t, low_t, pick_t = [mm(eye, v, 1, 1).astype(BF16) for v in (high, low, pick_f.astype(BF16))]
+        mixed_part = (mm(high_t, back_out) + mm(low_t, back_out)).astype(BF16)
+        gtok_part = mm(pick_t, back_in).astype(BF16)
+        inner = mm(back_out, cot_columns, 1, 1) * pick_f
+        inner = jnp.concatenate(
+            [jnp.sum(jnp.where(hits[k], inner, 0.0), axis=0, keepdims=True) for k in range(top)], axis=0
+        )
+        return gtok_part, mixed_part, inner
+
+    def halves(ref, half):
+        blocks = [ref[:, j].reshape(slots, LANE) for j in range(2 * half)]
+        return jnp.concatenate(blocks[:half], axis=1), jnp.concatenate(blocks[half:], axis=1)
+
+    for j in range(sb.slots):
         snd3[:, j] = ybuf[j].reshape(a_n, rows_a, LANE)
-    arrive(exchange("a", snd3, rcv3, s3, r3))
+    own = exchange("a", snd3, rcv3, s3, r3)
+    inners = []
+    if late:
+        for g in range(2):
+            arrive(back[g])
+            at = (kept + g * per_b) * LANE
+            order = (by_y, by_a)[g]
+            gtok_part, mixed_part, inner = at_home(order, *halves(rcv6.at[g], per_b), cot[:, at:at + per_b * LANE])
+            inners.append(inner)
+            for j in range(per_b):
+                tile = g * per_b + j
+                zsnd[tile, 0] = gtok_part[:, j * LANE:(j + 1) * LANE]
+                zsnd[n - late + tile, 1] = mixed_part[:, j * LANE:(j + 1) * LANE]
+        for o in range(n):
+            if o >= late:
+                zsnd[o, 0] = jnp.zeros((tok_n, LANE), BF16)
+            if o < n - late:
+                zsnd[o, 1] = jnp.zeros((tok_n, LANE), BF16)
+        over = []
+        for i in range(1, n):
+            o = lax.rem(z + i, n)
+            over.append(copy(zsnd.at[o], zrcv.at[z], zs.at[i], zr.at[i], (o, e)))
+        for c in over:
+            c.start()
+        zrcv[z] = zsnd[z]
+        sends.extend(over)
+    arrive(own)
     split_store(snd4, 0, regroup(rcv3, a_n, ny), ny)
-    arrive(exchange("y", snd4, rcv4, s4, r4))
-
-    back = [rcv4[:, j].reshape(slots, LANE) for j in range(sp.slots)]
-    back_in, back_out = jnp.concatenate(back[:size], axis=1), jnp.concatenate(back[size:], axis=1)
-    eye = jnp.where(iota((tok_n, tok_n), 0) == iota((tok_n, tok_n), 1), 1.0, 0.0).astype(BF16)
-    high = gate_of.astype(BF16)
-    low = (gate_of - high.astype(F32)).astype(BF16)
-    high_t, low_t, pick_t = [mm(eye, v, 1, 1).astype(BF16) for v in (high, low, pick)]
-    mixed_part = (mm(high_t, back_out) + mm(low_t, back_out)).astype(BF16)
-    gtok_part = mm(pick_t, back_in).astype(BF16)
-    shift = 1 if sp.extra else 0
-
-    def place(slot):
-        if slot < size:
-            return 0 if slot >= sp.base else slot + shift
-        return slot - size + sp.base + shift
-
+    own = exchange("y", snd4, rcv4, s4, r4)
+    if late:
+        arrive(over)
+        sums = [jnp.zeros((tok_n, LANE), F32)] * 2
+        for o in range(n):
+            for q in range(2):
+                sums[q] = sums[q] + zrcv[o, q].astype(F32)
+        fin[z, 0] = sums[0].astype(BF16)
+        fin[z, 2 * sb.base + 1] = sums[1].astype(BF16)
+    arrive(own)
+
+    gtok_part, mixed_part, inner = at_home(
+        by_y, *halves(rcv4, size), own_columns(sb, cot, 1, z)
+    )
+    for more in inners:
+        inner = inner + more
+    shift = 1 if late else 0
     for j in range(size):
-        fin[z, place(j)] = gtok_part[:, j * LANE:(j + 1) * LANE]
-        fin[z, place(size + j)] = mixed_part[:, j * LANE:(j + 1) * LANE]
-    inner = mm(back_out, own_columns(sp, cot, sp.second(z), sp.more_second), 1, 1) * pick_f
-    inner = jnp.concatenate(
-        [jnp.sum(jnp.where(hits[k], inner, 0.0), axis=0, keepdims=True) for k in range(top)], axis=0
-    )
+        fin[z, shift + j] = gtok_part[:, j * LANE:(j + 1) * LANE]
+        fin[z, shift + size + j] = mixed_part[:, j * LANE:(j + 1) * LANE]
     lane, line = iota((tok_n, LANE), 1), iota((tok_n, LANE), 0)
     spread = jnp.where((lane % tok_n == line) & (lane < top * tok_n), 1.0, 0.0)
     mine = iota((top, LANE), 1) // tok_n == iota((top, LANE), 0)
@@ -488,8 +570,13 @@
     total = jnp.zeros(gfin.shape[1:], F32)
     for o in range(n):
         total = total + gfin[o]
-        for slot, which, tile in sp.static(o):
-            (gtok, mixed)[which][:, tile * LANE:(tile + 1) * LANE] = fin[o, place(slot)]
+        held = [(shift + slot, which, tile) for slot, which, tile in sb.static(o)]
+        if late and o < late:
+            held.append((0, 0, kept + o))
+        if late and o >= n - late:
+            held.append((2 * sb.base + 1, 1, kept + o - (n - late)))
+        for slot, which, tile in held:
+            (gtok, mixed)[which][:, tile * LANE:(tile + 1) * LANE] = fin[o, slot]
     ggates[...] = exact(jnp.where(mine, total, 0.0), spread, 1)
 
     for c in sends:
@@ -497,9 +584,9 @@
     for way in range(2):
 
         def left_at(d, carry, way=way):
-            for split, pieces_copy, first in ((sd, gather_copy, 0), (sp, scatter_copy, 1)):
+            for split, pieces_copy, first, does in ((sd, gather_copy, 0, travels_in), (sb, scatter_copy, 1, travels)):
                 for p in range(len(split.pieces)):
-                    if travels(d + 1, way, split.group(p)):
+                    if does(d + 1, way, split.group(p)):
                         c, cond = pieces_copy(way, d + first, p)
                         when(cond, c.wait_send)
             return carry
@@ -510,6 +597,15 @@
         for c, cond in copies:
             when(cond, c.wait_send)
     store.wait()
+
+
+def hand_over(*refs):
+    sem = refs[8]
+    copies = [pltpu.make_async_copy(refs[i], refs[4 + i], sem.at[i]) for i in range(4)]
+    for c in copies:
+        c.start()
+    for c in copies:
+        c.wait()
 
 
 def local(n, n_expert, tokens, route, gate_code, cotangent, w_gate, w_up, w_down):
@@ -519,12 +615,16 @@
     ny, a_n = ROWS_Y, n_expert // ROWS_Y
     slots = n_expert * CAP
     tiles = width // LANE
-    direct = DIRECT if tiles > DIRECT else 0
-    sd, sp = Split(n, tiles - direct), Split(n, tiles)
-    k, np_ = sp.slots, len(sp.pieces)
+    direct = DIRECT if tiles > sum(DIRECT) else ()
+    m = n // 2 if n % 2 == 0 else n
+    sd, sp = Split(m, tiles - sum(direct)), Split(n, tiles)
+    late = sp.extra
+    sb = Split(n, tiles - late)
+    k, np_ = sb.slots, len(sb.pieces)
+    kb = max(1, late)
     kd, npd = sd.slots, len(sd.pieces)
-    groups, per2 = (GROUPS, 2 * direct // GROUPS) if direct else (1, 1)
-    hops = n // 2
+    groups, per2 = (2, 2 * max(direct)) if direct else (1, 1)
+    hops, hops_in = n // 2, m // 2
     vmem = pl.BlockSpec(memory_space=pltpu.VMEM)
     anyw = pl.BlockSpec(memory_space=pl.ANY)
     dma = pltpu.SemaphoreType.DMA
@@ -536,7 +636,7 @@
         return pltpu.VMEM(shape, F32)
 
     rows_y, rows_a = a_n * CAP, ny * CAP
-    mixed, gtok, ggates, gdown = pl.pallas_call(
+    results = pl.pallas_call(
         functools.partial(kernel, n, n_expert),
         out_shape=(
             jax.ShapeDtypeStruct((tok_n, width), BF16),
@@ -551,7 +651,7 @@
             b16(tok_n, width), b16(tok_n, width),
             b16(width + LANE, 2 * f), b16(f, width), b16(f, width),
             b16(ny, kd, rows_y, LANE), b16(ny, kd, rows_y, LANE), b16(a_n, kd, rows_a, LANE),
-            b16(n, kd, slots, LANE),
+            b16(m, kd, slots, LANE),
             b16(groups, ny, per2, rows_y, LANE), b16(groups, ny, per2, rows_y, LANE),
             b16(groups, a_n, per2, rows_a, LANE), b16(groups, per2, slots, LANE),
             f32(slots, 2 * f), f32(slots, f), f32(2, k, slots, LANE),
@@ -560,19 +660,31 @@
             b16(hops + 1, k, slots, LANE), b16(hops, k, slots, LANE),
             b16(k, slots, LANE), b16(a_n, k, rows_a, LANE), b16(a_n, k, rows_a, LANE),
             b16(ny, k, rows_y, LANE), b16(ny, k, rows_y, LANE),
-            b16(n, k, tok_n, LANE), f32(n, 1, LANE),
+            b16(2, a_n, kb, rows_a, LANE), b16(2, a_n, kb, rows_a, LANE),
+            b16(2, ny, kb, rows_y, LANE), b16(2, ny, kb, rows_y, LANE),
+            b16(n, 2, tok_n, LANE), b16(n, 2, tok_n, LANE),
+            b16(n, sp.slots, tok_n, LANE), f32(n, 1, LANE),
             dma((4,)), dma((3,)), dma((ny,)), dma((ny,)), dma((a_n,)), dma((a_n,)),
             dma((groups, ny)), dma((groups, ny)), dma((groups, a_n)), dma((groups, a_n)),
-            dma((2, hops, npd)), dma((2, hops + 1, npd)),
+            dma((2, hops_in, npd)), dma((2, hops_in + 1, npd)),
             dma((hops + 1, np_)), dma((hops, np_)), dma((hops + 1, np_)), dma((hops, np_)),
             dma((a_n,)), dma((a_n,)), dma((ny,)), dma((ny,)),
             dma((n, 2)), dma((n, 2)), dma,
+            dma((2, a_n)), dma((2, a_n)), dma((2, ny)), dma((2, ny)), dma((n,)), dma((n,)),
         ],
         compiler_params=pltpu.CompilerParams(
             collective_id=0, has_side_effects=True, vmem_limit_bytes=60 * 1024 * 1024
         ),
         name="moe_step",
     )(route.T, gate_code.T, tokens, cotangent, w_gate[0], w_up[0], w_down[0])
+    mixed, gtok, ggates, gdown = pl.pallas_call(
+        hand_over,
+        out_shape=tuple(jax.ShapeDtypeStruct(v.shape, v.dtype) for v in results),
+        in_specs=[vmem] * 4,
+        out_specs=(anyw,) * 4,
+        scratch_shapes=[dma((4,))],
+        name="hand_over",
+    )(*results)
     return mixed, gtok, ggates.T, gdown[None]
 
 

time: 110 us -> 102 us (0.927)
  local copies, waits for them, and re-layouts: 5.17 us -> 0 us
  Pallas kernels: 103 us -> 101 us
    unnamed x8 -> x0, local copies, waits for them, and re-layouts: 5.17 us -> none
    pallas_call x1, Pallas kernels: 103 us -> 98.5 us  [local(): pl.pallas_call(functools.partial(kernel, n, n_expert), out_shape=(jax.Sha...]
    pallas_call x0 -> x1, Pallas kernels: none -> 2.47 us  [local(): pl.pallas_call(hand_over, out_shape=tuple((jax.ShapeDtypeStruct(v.shape,...]
where the time goes in v4:
time: 102 us
  Pallas kernels  101 us (99%)
    pallas_call x1, Pallas kernels, local(): pl.pallas_call(functools.partial(kernel, n, n_expert), out_shape=(jax.Sha...  98.5 us
    pallas_call x1, Pallas kernels, local(): pl.pallas_call(hand_over, out_shape=tuple((jax.ShapeDtypeStruct(v.shape,...  2.47 us

profile of v4, /device:TPU:6, one launch (start us, length us, event | category | flops | bytes accessed | tf_op | source)
XLA Modules:
  0.0 101.6 jit_solution(1489513617374265875)
XLA Ops:
  0.6 98.5 %moe_step.1 = (bf16[16,4096]{1,0:T(8,128)(2,1)}, bf16[16,4096]{1,0:T(8,128)(2,1)}, f32[8,16]{1,0:T(8,128)}, bf16[128,4096]{1,0:T(8,128)(2,1)}) custom-call(s32[8,16]{1,0:T(8,128)} %bitcast.10, s32[8,16]{1,0:T(8,128)} %bitcast.11, bf16[16,4096]{1,0:T(8,128)(2,1)} %tokens_h.1, bf16[16,4096]{1,0:T(8,128)(2,1)} %cot_h.1, bf16[4096,128]{1,0:T(8,128)(2,1)} %bitcast.7, ...), custom_call_target="tpu_custom_call" | custom-call | tf_op jit(solution)/shard_map/moe_step/pallas_call | solution.py:639
  99.1 2.5 %hand_over.1 = (bf16[16,4096]{1,0:T(8,128)(2,1)}, bf16[16,4096]{1,0:T(8,128)(2,1)}, f32[8,16]{1,0:T(8,128)}, bf16[128,4096]{1,0:T(8,128)(2,1)}) custom-call(bf16[16,4096]{1,0:T(8,128)(2,1)} %get-tuple-element.12.refs_0_, bf16[16,4096]{1,0:T(8,128)(2,1)} %get-tuple-element.13.refs_1_, f32[8,16]{1,0:T(8,128)} %get-tuple-element.14.refs_2_, ...), custom_call_target="tpu_custom_call" | custom-call | tf_op jit(solution)/shard_map/hand_over/pallas_call | solution.py:680

commit v5 on v4

--- a/solution.py
+++ b/solution.py
@@ -14,7 +14,7 @@
 F32 = jnp.float32
 BF16 = jnp.bfloat16
 MESH = pl.DeviceIdType.MESH
-DIRECT = (4, 4)
+DIRECT = (4, 10)
 TURN = 1
 
 
@@ -211,7 +211,7 @@
         rows = pl.ds(pl.multiple_of(me * height, height), height)
         to = dst.at[:, rows] if by_rows else dst.at[me]
         copies = []
-        for i in range(1, count):
+        for i in sorted(range(1, count), key=lambda i: -min(i, count - i)):
             b, device = peer(i)
             copies.append(copy(src.at[b], to, ssem.at[i], rsem.at[i], device))
         for c in copies:
@@ -295,7 +295,7 @@
         at, count, cond = sd.pieces[p]
         block = gall.at[o, pl.ds(at, count)]
         to = d if arrival else d + 1
-        return copy(block, block, gs.at[way, d, p], gr.at[way, to, p], device), cond and cond(o)
+        return copy(block, block, gs.at[way, min(d, hops_in - 1), p], gr.at[way, to, p], device), cond and cond(o)
 
     def use_first(o):
         block = jnp.concatenate([gall[o, j] for j in range(sd.size)], axis=1)
@@ -355,7 +355,6 @@
     silu = gate_pre * sigma
     hidden = silu * up_pre
     hid[...] = hidden.astype(BF16)
-    hidt[...] = hidden.T.astype(BF16)
     ggu[:, :f] = (grad_hidden * up_pre * sigma * (1.0 + gate_pre * (1.0 - sigma))).astype(BF16)
     ggu[:, f:] = (grad_hidden * silu).astype(BF16)
 
@@ -427,6 +426,8 @@
         scatter_step(d)
         if late and d == hops:
             back_start()
+        if d == hops:
+            hidt[...] = hidden.T.astype(BF16)
         if late and d == max(1, hops - 2):
             back = [back_turn(0)]
         if late and d == max(1, hops - 4):

time: 102 us -> 99.2 us (0.973); the launches traced: 102 us -> 97.6 us
  Pallas kernels: 101 us -> 96.9 us
    pallas_call x1, Pallas kernels: 98.5 us -> 94.5 us  [local(): pl.pallas_call(functools.partial(kernel, n, n_expert), out_shape=(jax.Sha...]
where the time goes in v5:
time: 99.2 us; the launch traced here: 97.6 us
  Pallas kernels  96.9 us (98%)
    pallas_call x1, Pallas kernels, local(): pl.pallas_call(functools.partial(kernel, n, n_expert), out_shape=(jax.Sha...  94.5 us
    pallas_call x1, Pallas kernels, local(): pl.pallas_call(hand_over, out_shape=tuple((jax.ShapeDtypeStruct(v.shape,...  2.47 us

profile of v5, /device:TPU:6, one launch (start us, length us, event | category | flops | bytes accessed | tf_op | source)
XLA Modules:
  0.0 97.6 jit_solution(11373618659378753593)
XLA Ops:
  0.6 94.5 %moe_step.1 = (bf16[16,4096]{1,0:T(8,128)(2,1)}, bf16[16,4096]{1,0:T(8,128)(2,1)}, f32[8,16]{1,0:T(8,128)}, bf16[128,4096]{1,0:T(8,128)(2,1)}) custom-call(s32[8,16]{1,0:T(8,128)} %bitcast.10, s32[8,16]{1,0:T(8,128)} %bitcast.11, bf16[16,4096]{1,0:T(8,128)(2,1)} %tokens_h.1, bf16[16,4096]{1,0:T(8,128)(2,1)} %cot_h.1, bf16[4096,128]{1,0:T(8,128)(2,1)} %bitcast.7, ...), custom_call_target="tpu_custom_call" | custom-call | tf_op jit(solution)/shard_map/moe_step/pallas_call | solution.py:640
  95.1 2.5 %hand_over.1 = (bf16[16,4096]{1,0:T(8,128)(2,1)}, bf16[16,4096]{1,0:T(8,128)(2,1)}, f32[8,16]{1,0:T(8,128)}, bf16[128,4096]{1,0:T(8,128)(2,1)}) custom-call(bf16[16,4096]{1,0:T(8,128)(2,1)} %get-tuple-element.12.refs_0_, bf16[16,4096]{1,0:T(8,128)(2,1)} %get-tuple-element.13.refs_1_, f32[8,16]{1,0:T(8,128)} %get-tuple-element.14.refs_2_, ...), custom_call_target="tpu_custom_call" | custom-call | tf_op jit(solution)/shard_map/hand_over/pallas_call | solution.py:681
